TPU v7x, 256 devices: a whole 4x4x8 slice. The times are simulated.
256 devices in a mesh: mass: 8 (over x, core), seq: 32 (over y, z).
Axes of the slice: x: 4, y: 4, z: 8, core: 2. Of those that a mesh axis runs over, the one named last changes fastest.
Arguments:
- peptide_tokens: int32 [16384, 32], P(('mass', 'seq')), may hold values from 0 to 31
- peptide_lengths: int32 [16384], P(('mass', 'seq')), may hold values from 7 to 32
- target_owner: int32 [16384, 1], P(('mass', 'seq')), may hold values from 0 to 7; in each aligned block of 64 rows (0 to 63, 64 to 127, ...) at most 16 rows name the same one
- target_sub: int32 [16384], P(('mass', 'seq')), may hold values from 0 to 255
- decoy_owner: int32 [16384, 1], P(('mass', 'seq')), may hold values from 0 to 7; in each aligned block of 64 rows (0 to 63, 64 to 127, ...) at most 16 rows name the same one
- decoy_sub: int32 [16384], P(('mass', 'seq')), may hold values from 0 to 255
- embedding: bfloat16 [32, 256], replicated, may hold values from -6 to 6
- w_qkv: bfloat16 [2, 256, 768], replicated, may hold values from -2 to 2
- w_out: bfloat16 [2, 256, 256], replicated, may hold values from -0.375 to 0.375
- w_up: bfloat16 [2, 256, 1024], replicated, may hold values from -0.375 to 0.375
- w_down: bfloat16 [2, 1024, 256], replicated, may hold values from -0.1875 to 0.1875
- layer_gain: bfloat16 [2, 2, 256], replicated, may hold values from 0.5 to 1.5
- final_gain: bfloat16 [256], replicated, may hold values from 0.5 to 1.5
- w_head: bfloat16 [256, 32], replicated, may hold values from -0.375 to 0.375
- query_spectra: bfloat16 [8192, 1024], P(('mass', 'seq')), may hold values from -6 to 6
- query_bin: int32 [8192], P(('mass', 'seq')), may hold values from 0 to 2047, as said below
Outputs:
- target_best: float32 [8192], P(('mass', 'seq'))
- decoy_best: float32 [8192], P(('mass', 'seq'))
Inputs may be any that keep to these rules, and one draw needn't show every extreme that they name: `target_owner`: among the rows of one device at most 16 name the same owner. `decoy_owner`: among the rows of one device at most 16 name the same owner. `query_bin`: queries d * 32 to (d + 1) * 32 - 1 hold the bins d * 8 to (d + 1) * 8 - 1, each exactly 4 times.
All inputs are finite; a program needn't handle non-finite values.
Results may differ from a plain program's by a relative error of at most 0.0055.
Values may be sent and summed in bfloat16 or wider, within the bound.
No kernel may reach another device: no remote copies, remote signals or barrier semaphores. Data moves between devices by JAX's collectives and lax.ppermute only.
A program may use at most 128 MiB of HBM per device.

v0:
```python
import functools
import math

import jax
import jax.numpy as jnp
import numpy as np
from jax import lax
from jax.experimental import pallas as pl
from jax.experimental.pallas import tpu as pltpu
from jax.sharding import PartitionSpec as P

HEADS = 8
L = 32
ION = 32
NL = 2
QPB = 4
YS = 4
D = 256
FF = 1024
SPEC = L * ION
EPS = 1e-06
BF = jnp.bfloat16
F32 = jnp.float32

STEP = 1024
TILE = 128
GROUP = 8
PIECES = 1
ROWW = SPEC + 128
VMEM_LIMIT = 60 * 1024 * 1024
NT = (((1,), (1,)), ((), ()))


def sinusoid():
    place = np.arange(L, dtype=np.float32)[:, None]
    index = np.arange(D // 2, dtype=np.float32)[None, :]
    angle = place * np.exp(-math.log(10000.0) * 2.0 * index / D).astype(np.float32)
    return np.concatenate([np.sin(angle), np.cos(angle)], axis=1).astype(np.float32)


def lane_iota(shape):
    return lax.broadcasted_iota(jnp.int32, shape, len(shape) - 1)


def row_iota(shape):
    return lax.broadcasted_iota(jnp.int32, shape, len(shape) - 2)


def norm_rows(values, gain):
    scale = lax.rsqrt(jnp.mean(values * values, axis=-1, keepdims=True) + EPS)
    return (values * scale * gain).astype(BF)


def standardize(spectra):
    centred = spectra - jnp.mean(spectra, axis=-1, keepdims=True)
    return (centred * lax.rsqrt(jnp.mean(centred * centred, axis=-1, keepdims=True) + EPS)).astype(BF)


def gelu(x):
    inner = x * (math.sqrt(2 / math.pi) + (math.sqrt(2 / math.pi) * 0.044715) * (x * x))
    half = 0.5 * x
    return half + half * jnp.tanh(inner)


def feed_forward(state, normed, w_up_ref, w_down_ref):
    for c in range(0, FF, D):
        up = jnp.dot(normed, w_up_ref[:, c : c + D], preferred_element_type=F32)
        hidden = gelu(up).astype(BF)
        state = state + jnp.dot(hidden, w_down_ref[c : c + D, :], preferred_element_type=F32)
    return state


def attend(items):
    heads, peps = TILE // L, TILE // L
    lane = (lane_iota((L, heads * TILE)) % TILE) // L
    empty = jnp.zeros((L, TILE), BF)
    scores = []
    for query, key, _, _ in items:
        turned = query.T
        spread = [
            jnp.concatenate(
                [turned[h * L : (h + 1) * L] if h == i else empty for i in range(heads)], axis=1
            )
            for h in range(heads)
        ]
        spread = jnp.concatenate(spread, axis=0)
        scores.append(jnp.dot(key, spread, preferred_element_type=F32))
    wide = []
    for score, (_, _, _, length) in zip(scores, items):
        own = score[:L]
        for j in range(1, peps):
            own = jnp.where(lane == j, score[j * L : (j + 1) * L], own)
        own = own * (1.0 / math.sqrt(L))
        own = jnp.where(
            row_iota(own.shape) < jnp.concatenate([length] * heads, axis=1), own, F32(-1e30)
        )
        weights = jnp.exp(own - jnp.max(own, axis=0, keepdims=True))
        probs = weights * (1.0 / jnp.sum(weights, axis=0, keepdims=True))
        probs = probs.astype(BF)
        wide.append(
            jnp.concatenate(
                [jnp.where(lane == j, probs, jnp.zeros_like(probs)) for j in range(peps)], axis=0
            )
        )
    heard = []
    for probs, (_, _, value, _) in zip(wide, items):
        turned = value.T
        heard.append(
            jnp.concatenate(
                [
                    jnp.dot(
                        turned[h * L : (h + 1) * L],
                        probs[:, h * TILE : (h + 1) * TILE],
                        preferred_element_type=F32,
                    )
                    for h in range(heads)
                ],
                axis=0,
            )
        )
    return [out.T.astype(BF) for out in heard]


def predict_kernel(
    base,
    lengths_ref,
    towner_ref,
    tsub_ref,
    downer_ref,
    dsub_ref,
    tokens_ref,
    embedding_ref,
    code_ref,
    w_qkv_ref,
    w_out_ref,
    w_up_ref,
    w_down_ref,
    gain_ref,
    final_ref,
    w_head_ref,
    *refs,
):
    rows_ref, logit_ref, sems = refs[-7], refs[-6], refs[-1]
    peps = STEP // L
    sources = (w_qkv_ref, w_out_ref, w_up_ref, w_down_ref)
    kept = refs[-5:-1]
    moves = [
        [
            pltpu.make_async_copy(
                source.at[layer, pl.ds(p * source.shape[1] // PIECES, source.shape[1] // PIECES)],
                held.at[layer, pl.ds(p * source.shape[1] // PIECES, source.shape[1] // PIECES)],
                sems.at[layer, i, p],
            )
            for i, (source, held) in enumerate(zip(sources, kept))
            for p in range(PIECES)
        ]
        for layer in range(NL)
    ]
    w_qkv_ref, w_out_ref, w_up_ref, w_down_ref = kept
    for move in moves[0] + moves[1]:
        move.start()

    first = base
    tokens = tokens_ref[...]
    tokens = jnp.concatenate([tokens] * (128 // tokens.shape[1]), axis=1)
    tokens = pltpu.roll(tokens, (128 - first) % 128, 1)
    vocab = embedding_ref.shape[0]
    onehot = jnp.concatenate(
        [tokens[:, j : j + 1] == lane_iota((L, vocab)) for j in range(peps)], axis=0
    ).astype(BF)
    state = jnp.dot(onehot, embedding_ref[...], preferred_element_type=F32)
    state = state + jnp.concatenate([code_ref[...]] * peps, axis=0)

    tile_lengths = []
    for t in range(STEP // TILE):
        lane = lane_iota((1, TILE)) // L
        vec = jnp.full((1, TILE), lengths_ref[first + t * 4], jnp.int32)
        for j in range(1, TILE // L):
            vec = jnp.where(lane == j, lengths_ref[first + t * 4 + j], vec)
        tile_lengths.append(vec)

    for layer in range(NL):
        normed = norm_rows(state, gain_ref[layer, 0:1, :].astype(F32))
        for move in moves[layer]:
            move.wait()
        mixed = [
            jnp.dot(
                normed, w_qkv_ref[layer, :, c * D : (c + 1) * D], preferred_element_type=F32
            ).astype(BF)
            for c in range(3)
        ]
        items = [
            [m[t * TILE : (t + 1) * TILE, g * TILE : (g + 1) * TILE] for m in mixed] + [tile_lengths[t]]
            for t in range(STEP // TILE)
            for g in range(D // TILE)
        ]
        heard = []
        for i in range(0, len(items), GROUP):
            heard = heard + attend(items[i : i + GROUP])
        attended = jnp.concatenate(
            [jnp.concatenate(heard[i : i + 2], axis=1) for i in range(0, len(heard), 2)], axis=0
        )
        state = state + jnp.dot(attended, w_out_ref[layer], preferred_element_type=F32)
        normed = norm_rows(state, gain_ref[layer, 1:2, :].astype(F32))
        state = feed_forward(state, normed, w_up_ref.at[layer], w_down_ref.at[layer])
    normed = norm_rows(state, final_ref[...].reshape(1, D).astype(F32))
    head = jnp.concatenate([w_head_ref[...]] * 4, axis=0)
    logit_ref[...] = lax.dot_general(normed, head, NT, preferred_element_type=F32)

    lane = lane_iota((peps, 128)) // ION
    tiles = []
    for t in range(SPEC // 128):
        tile = logit_ref[pl.ds(4 * t, peps, stride=L), :]
        for i in range(1, 4):
            tile = jnp.where(lane == i, logit_ref[pl.ds(4 * t + i, peps, stride=L), :], tile)
        tiles.append(tile)
    logits = jnp.concatenate(tiles, axis=1)
    intensity = 1.0 / (1.0 + jnp.exp(-logits))
    row = row_iota((peps, 128))
    column = lane_iota((peps, 128))
    length = jnp.zeros((peps, 128), jnp.int32)
    tag = jnp.zeros((peps, 128), jnp.int32)
    for i in range(peps):
        length = jnp.where(row == i, lengths_ref[first + i], length)
        for c, ref in enumerate((towner_ref, tsub_ref, downer_ref, dsub_ref)):
            tag = jnp.where((row == i) & (column == c), ref[first + i], tag)
    position = lane_iota((peps, SPEC)) // ION
    length = jnp.concatenate([length] * (SPEC // 128), axis=1)
    intensity = jnp.where(position < length - 1, intensity, F32(0.0))
    rows_ref[:, :SPEC] = standardize(intensity)
    rows_ref[:, SPEC:] = tag.astype(F32).astype(BF)


def predict_rows(
    part,
    parts,
    before,
    tokens,
    lengths,
    towner,
    tsub,
    downer,
    dsub,
    embedding,
    w_qkv,
    w_out,
    w_up,
    w_down,
    gains,
    final,
    w_head,
):
    count = tokens.shape[0]
    peps = STEP // L
    assert parts * peps == count
    whole = lambda shape: pl.BlockSpec(shape, lambda i, *_: (0,) * len(shape))
    operands = (
        tokens.T,
        embedding,
        jnp.asarray(sinusoid()),
        w_qkv,
        w_out,
        w_up,
        w_down,
        gains,
        final,
        w_head.T,
    )
    large = (w_qkv, w_out, w_up, w_down)
    in_specs = [
        pl.BlockSpec(memory_space=pltpu.HBM) if operand.ndim == 3 and operand is not gains else whole(operand.shape)
        for operand in operands
    ]
    scalars = (lengths, towner.reshape(count), tsub, downer.reshape(count), dsub)
    aliases = {}
    if before is not None:
        aliases = {len(scalars) + len(operands): 0}
        operands += (before,)
        in_specs += [pl.BlockSpec(memory_space=pl.ANY)]
    grid = pltpu.PrefetchScalarGridSpec(
        num_scalar_prefetch=len(scalars),
        grid=(1,),
        in_specs=in_specs,
        out_specs=pl.BlockSpec((peps, ROWW), lambda i, *_: (part, 0)),
        scratch_shapes=[pltpu.VMEM((STEP, 128), F32)]
        + [pltpu.VMEM(weight.shape, BF) for weight in large]
        + [pltpu.SemaphoreType.DMA((NL, len(large), PIECES))],
    )
    tokens_here = count * L // parts
    return pl.pallas_call(
        functools.partial(predict_kernel, part * peps),
        grid_spec=grid,
        out_shape=jax.ShapeDtypeStruct((count, ROWW), BF),
        input_output_aliases=aliases,
        compiler_params=pltpu.CompilerParams(vmem_limit_bytes=VMEM_LIMIT),
        cost_estimate=pl.CostEstimate(
            flops=2 * 12 * NL * tokens_here * D * D,
            bytes_accessed=4 * 2**20,
            transcendentals=2 * tokens_here * FF,
        ),
        name="predict",
    )(*scalars, *operands)


def slots_of(bins):
    count = bins.shape[1]
    across = jnp.broadcast_to(bins.astype(F32), (count, count))
    down = across.T
    earlier = (across == down) & (row_iota((count, count)) < lane_iota((count, count)))
    rank = jnp.sum(earlier.astype(F32), axis=0, keepdims=True)
    local = bins.astype(F32) - jnp.min(bins.astype(F32), axis=1, keepdims=True)
    return (local * QPB + rank).astype(jnp.int32)


def query_kernel(copies, bins_ref, spectra_ref, out_ref, ready_ref, sem):
    count = spectra_ref.shape[0]
    place = (row_iota((count, count)) == slots_of(bins_ref[...])).astype(BF)
    ready = standardize(spectra_ref[...].astype(F32))
    ready_ref[...] = jnp.dot(place, ready, preferred_element_type=F32).astype(BF)
    moves = [pltpu.make_async_copy(ready_ref, out_ref.at[i], sem.at[i]) for i in range(copies)]
    for move in moves:
        move.start()
    for move in moves:
        move.wait()


def prepare_queries(query_bin, spectra, copies):
    count = spectra.shape[0]
    return pl.pallas_call(
        functools.partial(query_kernel, copies),
        out_shape=jax.ShapeDtypeStruct((copies,) + spectra.shape, BF),
        out_specs=pl.BlockSpec(memory_space=pltpu.HBM),
        scratch_shapes=[pltpu.VMEM(spectra.shape, BF), pltpu.SemaphoreType.DMA((copies,))],
        compiler_params=pltpu.CompilerParams(vmem_limit_bytes=VMEM_LIMIT),
        name="prepare",
    )(query_bin.reshape(1, count), spectra)


def turn_kernel(mass_ref, *refs):
    sources, (side_ref, subs_ref) = refs[:-2], refs[-2:]
    count = sources[0].shape[0]
    per = 128 // count
    half = len(sources) * count
    me = mass_ref[0].astype(F32)
    for i in range(len(sources) // per):
        group = sources[i * per : (i + 1) * per]
        turned = jnp.concatenate([ref[:, :SPEC] for ref in group], axis=0).T
        lanes = pl.ds(i * 128, 128)
        side_ref[:, lanes] = turned
        for p in range(L):
            side_ref[p * ION : (p + 1) * ION, pl.ds(half + i * 128, 128)] = turned[
                (L - 1 - p) * ION : (L - p) * ION
            ]
        tags = jnp.concatenate([ref[:, SPEC:] for ref in group], axis=0).astype(F32).T
        for kind in range(2):
            owner, sub = tags[2 * kind : 2 * kind + 1], tags[2 * kind + 1 : 2 * kind + 2]
            sub = jnp.where(owner == me, sub, F32(-1.0))
            subs_ref[:, pl.ds(kind * half + i * 128, 128)] = jnp.broadcast_to(sub, (8, 128))


def turn(mass, sources):
    columns = 2 * len(sources) * sources[0].shape[0]
    return pl.pallas_call(
        turn_kernel,
        in_specs=[pl.BlockSpec(memory_space=pltpu.SMEM)]
        + [pl.BlockSpec(memory_space=pltpu.VMEM)] * len(sources),
        out_shape=(
            jax.ShapeDtypeStruct((SPEC, columns), BF),
            jax.ShapeDtypeStruct((8, columns), F32),
        ),
        compiler_params=pltpu.CompilerParams(vmem_limit_bytes=32 * 1024 * 1024),
        cost_estimate=pl.CostEstimate(flops=0, bytes_accessed=4 * 2**20, transcendentals=0),
        name="turn",
    )(mass, *sources)


def score_kernel(zs, seq_ref, side_ref, subs_ref, *refs):
    blocks, out_ref = refs[:-1], refs[-1]
    half = side_ref.shape[1] // 2
    y = lax.div(seq_ref[0], zs)
    low, row = lane_iota((8, 128)) < 32, row_iota((8, 128))
    for back, block in enumerate(blocks):
        queries = block[...]
        count = queries.shape[0]
        there = lax.rem(y + len(blocks) - back, len(blocks))
        bins = (row_iota((count, 128)) // QPB + there * (count // QPB)).astype(F32)
        best = []
        for kind in range(2):
            scores = jnp.dot(
                queries, side_ref[:, kind * half : (kind + 1) * half], preferred_element_type=F32
            )
            top = jnp.zeros((count, 128), F32)
            for i in range(half // 128):
                sub = subs_ref[:1, kind * half + i * 128 : kind * half + (i + 1) * 128]
                top = jnp.maximum(
                    top, jnp.where(sub == bins, scores[:, i * 128 : (i + 1) * 128], F32(0.0))
                )
            best.append(jnp.max(top.T, axis=0, keepdims=True) * F32(1.0 / math.sqrt(SPEC)))
        out = jnp.zeros((8, 128), F32)
        for z in range(zs):
            tile, shift = z // 4, 32 * (z % 4)
            pair = [jnp.broadcast_to(b[:, tile * 128 : (tile + 1) * 128], (8, 128)) for b in best]
            near = pltpu.roll(pair[0], (128 - shift) % 128, 1)
            far = pltpu.roll(pair[1], (128 - shift + 32) % 128, 1)
            out = jnp.where(row == z, jnp.where(low, near, far), out)
        out_ref[pl.ds(pl.multiple_of(there * zs, 8), zs), :] = out


def score(zs, seq, side, subs, blocks):
    inside = pl.BlockSpec(memory_space=pltpu.VMEM)
    queries = len(blocks) * blocks[0].shape[0]
    return pl.pallas_call(
        functools.partial(score_kernel, zs),
        in_specs=[pl.BlockSpec(memory_space=pltpu.SMEM)] + [inside] * (2 + len(blocks)),
        out_specs=inside,
        out_shape=jax.ShapeDtypeStruct((queries // 32, 128), F32),
        compiler_params=pltpu.CompilerParams(vmem_limit_bytes=32 * 1024 * 1024),
        name="score",
    )(seq, side, subs, *blocks)


def finish_kernel(bins_ref, pieces_ref, target_ref, decoy_ref):
    count = bins_ref.shape[1]
    best = jnp.maximum(jnp.max(pieces_ref[...], axis=0, keepdims=True), F32(0.0))
    slots = slots_of(bins_ref[...])
    place = row_iota((count, count)) == slots
    for kind, ref in enumerate((target_ref, decoy_ref)):
        wide = jnp.broadcast_to(best[:, kind * count : (kind + 1) * count], (count, count)).T
        ref[...] = jnp.sum(jnp.where(place, wide, F32(0.0)), axis=0, keepdims=True)


def finish(query_bin, pieces):
    count = query_bin.shape[0]
    shape = jax.ShapeDtypeStruct((1, count), F32)
    target, decoy = pl.pallas_call(finish_kernel, out_shape=(shape, shape), name="finish")(
        query_bin.reshape(1, count), pieces
    )
    return target.reshape(count), decoy.reshape(count)


def local(
    peptide_tokens,
    peptide_lengths,
    target_owner,
    target_sub,
    decoy_owner,
    decoy_sub,
    embedding,
    w_qkv,
    w_out,
    w_up,
    w_down,
    layer_gain,
    final_gain,
    w_head,
    query_spectra,
    query_bin,
):
    seqs = lax.axis_size("seq")
    ys, zs = YS, seqs // YS
    along_z = [[y * zs + z for z in range(zs)] for y in range(ys)]
    weights = (embedding, w_qkv, w_out, w_up, w_down, layer_gain, final_gain, w_head)
    owners = (target_owner, target_sub, decoy_owner, decoy_sub)
    queries = prepare_queries(query_bin, query_spectra, zs)
    queries = lax.all_to_all(
        queries, "seq", split_axis=0, concat_axis=0, tiled=True, axis_index_groups=along_z
    ).reshape(-1, SPEC)
    rows = predict_rows(0, 2, None, peptide_tokens, peptide_lengths, *owners, *weights)
    queries, rows, peptide_lengths = lax.optimization_barrier((queries, rows, peptide_lengths))
    ahead, back = [[(i, (i + d * zs) % seqs) for i in range(seqs)] for d in (1, ys - 1)]
    blocks = [queries, lax.ppermute(queries, "seq", ahead), None, lax.ppermute(queries, "seq", back)]
    rows = predict_rows(1, 2, rows, peptide_tokens, peptide_lengths, *owners, *weights)
    rows, blocks[1], blocks[3] = lax.optimization_barrier((rows, blocks[1], blocks[3]))
    blocks[2] = lax.ppermute(blocks[1], "seq", ahead)
    masses = lax.axis_size("mass")
    swap = [(i, i ^ 1) for i in range(masses)]
    held = [rows] + [
        lax.ppermute(rows, "mass", [(i, (i + d) % masses) for i in range(masses)])
        for d in range(2, masses, 2)
    ]
    held = held + [lax.ppermute(part, "mass", swap) for part in held]
    mass, seq = [lax.axis_index(axis).astype(jnp.int32).reshape(1) for axis in ("mass", "seq")]
    side, subs = turn(mass, held)
    pieces = score(zs, seq, side, subs, blocks)[:, None, :]
    pieces = lax.all_to_all(pieces, "seq", split_axis=0, concat_axis=0, tiled=True)[:, 0, :]
    return finish(query_bin, pieces)


def solution(mesh):
    in_specs = (
        P(("mass", "seq"), None),
        P(("mass", "seq")),
        P(("mass", "seq"), None),
        P(("mass", "seq")),
        P(("mass", "seq"), None),
        P(("mass", "seq")),
        P(),
        P(),
        P(),
        P(),
        P(),
        P(),
        P(),
        P(),
        P(("mass", "seq"), None),
        P(("mass", "seq")),
    )
    out_specs = (P(("mass", "seq")), P(("mass", "seq")))
    return jax.shard_map(local, mesh=mesh, in_specs=in_specs, out_specs=out_specs, check_vma=False)
```

profile of v0, /device:TPU:1, one launch (start us, length us, event | category | flops | bytes accessed | tf_op | source)
XLA Modules:
  0.0 76.2 jit_solution(3907249483352134800)
XLA Ops:
  0.6 2.1 %prepare.1 = bf16[8,32,1024]{2,1,0:T(8,128)(2,1)} custom-call(s32[1,32]{1,0:T(1,128)} %bitcast.19, bf16[32,1024]{1,0:T(8,128)(2,1)} %spectra_ref.1), custom_call_target="tpu_custom_call" | custom-call | tf_op jit(solution)/shard_map/prepare/pallas_call | solution.py:329
  2.7 9.0 %all-to-all-start = ((bf16[8,32,1024]{2,1,0:T(8,128)(2,1)}), bf16[8,32,1024]{2,1,0:T(8,128)(2,1)S(1)}, u32[]{:S(2)}, u32[]{:S(2)}) async-start(bf16[8,32,1024]{2,1,0:T(8,128)(2,1)} %prepare.1), calls=%async_computation | async-start | bytes 1048576 | tf_op jit(solution)/shard_map/all_to_all | solution.py:465
  11.7 11.6 %predict.2.refs_0_ = bf16[64,1152]{1,0:T(8,128)(2,1)} custom-call(s32[64]{0:T(128)} %lengths_ref.2, s32[64]{0:T(128)} %bitcast.25, s32[64]{0:T(128)} %tsub_ref.3, s32[64]{0:T(128)} %bitcast.27, s32[64]{0:T(128)} %dsub_ref.3, s32[32,64]{1,0:T(8,128)} %bitcast.21, bf16[32,256]{1,0:T(8,128)(2,1)} %embedding_ref.3, f32[32,256]{1,0:T(8,128)} %constant.11.clone.code_ref, ...), custom_call_target="tpu_custom_call" | custom-call | flops 3221225472 | bytes 4194304 | tf_op jit(solution)/shard_map/predict/pallas_call | solution.py:290
  23.3 6.4 %all-to-all-done = bf16[8,32,1024]{2,1,0:T(8,128)(2,1)S(1)} async-done(((bf16[8,32,1024]{2,1,0:T(8,128)(2,1)}), bf16[8,32,1024]{2,1,0:T(8,128)(2,1)S(1)}, u32[]{:S(2)}, u32[]{:S(2)}) %all-to-all-start) | async-done | bytes 524320 | tf_op jit(solution)/shard_map/all_to_all | solution.py:465
  29.7 1.3 %collective-permute-start = (bf16[256,1024]{1,0:T(8,128)(2,1)S(1)}, bf16[256,1024]{1,0:T(8,128)(2,1)S(1)}, u32[]{:S(2)}, u32[]{:S(2)}) collective-permute-start(bf16[256,1024]{1,0:T(8,128)(2,1)S(1)} %bitcast.14), channel_id=1, source_target_pairs={{0,8},{1,9},{2,10},{3,11},{4,12},{5,13},{6,14},{7,15},{8,16},{9,17... | collective-permute-start | bytes 1572872 | tf_op jit(solution)/shard_map/ppermute | solution.py:471
  31.0 1.4 %collective-permute-start.1 = (bf16[256,1024]{1,0:T(8,128)(2,1)S(1)}, bf16[256,1024]{1,0:T(8,128)(2,1)S(1)}, u32[]{:S(2)}, u32[]{:S(2)}) collective-permute-start(bf16[256,1024]{1,0:T(8,128)(2,1)S(1)} %bitcast.15), channel_id=1, source_target_pairs={{0,24},{1,25},{2,26},{3,27},{4,28},{5,29},{6,30},{7,31},{8,0},{9,1... | collective-permute-start | bytes 1572872 | tf_op jit(solution)/shard_map/ppermute | solution.py:471
  32.4 11.6 %predict.3.refs_0_ = bf16[64,1152]{1,0:T(8,128)(2,1)} custom-call(s32[64]{0:T(128)} %lengths_ref.2, s32[64]{0:T(128)} %bitcast.26, s32[64]{0:T(128)} %tsub_ref.3, s32[64]{0:T(128)} %bitcast.28, s32[64]{0:T(128)} %dsub_ref.3, s32[32,64]{1,0:T(8,128)} %bitcast.22, bf16[32,256]{1,0:T(8,128)(2,1)} %embedding_ref.3, ...), custom_call_target="tpu_custom_call", output_to_operand_aliasing={{}: (15, {})} | custom-call | flops 3221225472 | bytes 4194304 | tf_op jit(solution)/shard_map/predict/pallas_call | solution.py:290
  44.0 0.0 collective-permute-done.refs_1_
  44.0 0.0 collective-permute-done.1.refs_3_
  44.0 0.9 %collective-permute-start.9 = (bf16[256,1024]{1,0:T(8,128)(2,1)S(1)}, bf16[256,1024]{1,0:T(8,128)(2,1)S(1)}, u32[]{:S(2)}, u32[]{:S(2)}) collective-permute-start(bf16[256,1024]{1,0:T(8,128)(2,1)S(1)} %collective-permute-done.refs_1_), channel_id=1, source_target_pairs={{0,8},{1,9},{2,10},{3,11},{4,12},{5,13},{6,14},{7,15},{8,16},{9,17... | collective-permute-start | bytes 1572872 | tf_op jit(solution)/shard_map/ppermute | solution.py:474
  45.0 1.2 %collective-permute-start.2 = (bf16[64,1152]{1,0:T(8,128)(2,1)}, bf16[64,1152]{1,0:T(8,128)(2,1)S(1)}, u32[]{:S(2)}, u32[]{:S(2)}) collective-permute-start(bf16[64,1152]{1,0:T(8,128)(2,1)} %predict.3.refs_0_), channel_id=1, source_target_pairs={{0,64},{32,96},{64,128},{96,160},{128,192},{160,224},{192,0},{224,... | collective-permute-start | bytes 442376 | tf_op jit(solution)/shard_map/ppermute | solution.py:478
  46.2 2.4 %collective-permute-start.3 = (bf16[64,1152]{1,0:T(8,128)(2,1)}, bf16[64,1152]{1,0:T(8,128)(2,1)S(1)}, u32[]{:S(2)}, u32[]{:S(2)}) collective-permute-start(bf16[64,1152]{1,0:T(8,128)(2,1)} %predict.3.refs_0_), channel_id=1, source_target_pairs={{0,128},{32,160},{64,192},{96,224},{128,0},{160,32},{192,64},{224,... | collective-permute-start | bytes 442376 | tf_op jit(solution)/shard_map/ppermute | solution.py:478
  48.6 1.2 %collective-permute-start.4 = (bf16[64,1152]{1,0:T(8,128)(2,1)}, bf16[64,1152]{1,0:T(8,128)(2,1)S(1)}, u32[]{:S(2)}, u32[]{:S(2)}) collective-permute-start(bf16[64,1152]{1,0:T(8,128)(2,1)} %predict.3.refs_0_), channel_id=1, source_target_pairs={{0,192},{32,224},{64,0},{96,32},{128,64},{160,96},{192,128},{224,1... | collective-permute-start | bytes 442376 | tf_op jit(solution)/shard_map/ppermute | solution.py:478
  49.8 2.8 %collective-permute-start.5 = (bf16[64,1152]{1,0:T(8,128)(2,1)}, bf16[64,1152]{1,0:T(8,128)(2,1)S(1)}, u32[]{:S(2)}, u32[]{:S(2)}) collective-permute-start(bf16[64,1152]{1,0:T(8,128)(2,1)} %predict.3.refs_0_), channel_id=1, source_target_pairs={{0,32},{32,0},{64,96},{96,64},{128,160},{160,128},{192,224},{224,1... | collective-permute-start | bytes 442376 | tf_op jit(solution)/shard_map/ppermute | solution.py:481
  52.6 0.0 collective-permute-done.2.refs_1_
  52.6 2.5 %collective-permute-start.6 = (bf16[64,1152]{1,0:T(8,128)(2,1)S(1)}, bf16[64,1152]{1,0:T(8,128)(2,1)S(1)}, u32[]{:S(2)}, u32[]{:S(2)}) collective-permute-start(bf16[64,1152]{1,0:T(8,128)(2,1)S(1)} %collective-permute-done.2.refs_1_), channel_id=1, source_target_pairs={{0,32},{32,0},{64,96},{96,64},{128,160},{160,128},{192,224},{224,1... | collective-permute-start | bytes 442376 | tf_op jit(solution)/shard_map/ppermute | solution.py:481
  55.0 0.0 collective-permute-done.3.refs_2_
  55.1 1.7 %collective-permute-start.7 = (bf16[64,1152]{1,0:T(8,128)(2,1)S(1)}, bf16[64,1152]{1,0:T(8,128)(2,1)S(1)}, u32[]{:S(2)}, u32[]{:S(2)}) collective-permute-start(bf16[64,1152]{1,0:T(8,128)(2,1)S(1)} %collective-permute-done.3.refs_2_), channel_id=1, source_target_pairs={{0,32},{32,0},{64,96},{96,64},{128,160},{160,128},{192,224},{224,1... | collective-permute-start | bytes 442376 | tf_op jit(solution)/shard_map/ppermute | solution.py:481
  56.8 0.0 collective-permute-done.4.refs_3_
  56.8 0.0 collective-permute-start.8
  56.8 0.0 collective-permute-done.5.refs_4_
  56.8 0.0 collective-permute-done.6.refs_5_
  56.8 1.0 %collective-permute-done.7.refs_6_ = bf16[64,1152]{1,0:T(8,128)(2,1)S(1)} collective-permute-done((bf16[64,1152]{1,0:T(8,128)(2,1)S(1)}, bf16[64,1152]{1,0:T(8,128)(2,1)S(1)}, u32[]{:S(2)}, u32[]{:S(2)}) %collective-permute-start.7) | collective-permute-done | bytes 147488 | tf_op jit(solution)/shard_map/ppermute | solution.py:481
  57.8 0.4 collective-permute-done.8.refs_7_
  58.2 0.0 copy-start
  58.2 0.9 %copy-done = bf16[64,1152]{1,0:T(8,128)(2,1)S(1)} copy-done((bf16[64,1152]{1,0:T(8,128)(2,1)S(1)}, bf16[64,1152]{1,0:T(8,128)(2,1)}, u32[]{:S(2)}) %copy-start) | copy-done | bytes 147480
  59.1 0.4 turn.1
  59.5 0.0 collective-permute-done.9.refs_2_
  59.5 2.5 %score.1 = f32[32,128]{1,0:T(8,128)S(1)} custom-call(s32[1]{0:T(128)} %bitcast.1.seq_ref, bf16[1024,1024]{1,0:T(8,128)(2,1)S(1)} %get-tuple-element.16.side_ref, f32[8,1024]{1,0:T(8,128)S(1)} %get-tuple-element.17.subs_ref, bf16[256,1024]{1,0:T(8,128)(2,1)S(1)} %bitcast.16, bf16[256,1024]{1,0:T(8,128)(2,1)S(1)} %collective-permute-done.refs_1_, ...), custom_call_target="tpu_custom_call" | custom-call | tf_op jit(solution)/shard_map/score/pallas_call | solution.py:412
  62.0 12.8 %all_to_all.10 = f32[32,1,128]{2,1,0:T(1,128)} all-to-all(f32[32,1,128]{2,1,0:T(1,128)S(1)} %bitcast.17), channel_id=1, replica_groups=mesh['mass'=8,'seq'=32] {'seq'}, dimensions={0} | all-to-all | bytes 32768 | tf_op jit(solution)/shard_map/all_to_all | solution.py:485
  74.8 1.4 %finish.1 = (f32[1,32]{1,0:T(1,128)}, f32[1,32]{1,0:T(1,128)}) custom-call(s32[1,32]{1,0:T(1,128)} %bitcast.20, f32[32,128]{1,0:T(8,128)} %bitcast.18), custom_call_target="tpu_custom_call" | custom-call | tf_op jit(solution)/shard_map/finish/pallas_call | solution.py:435
Async XLA Ops:
  2.7 27.0 %all-to-all-start = ((bf16[8,32,1024]{2,1,0:T(8,128)(2,1)}), bf16[8,32,1024]{2,1,0:T(8,128)(2,1)S(1)}, u32[]{:S(2)}, u32[]{:S(2)}) async-start(bf16[8,32,1024]{2,1,0:T(8,128)(2,1)} %prepare.1), calls=%async_computation | async-start | bytes 1048576 | tf_op jit(solution)/shard_map/all_to_all | solution.py:465
  29.7 14.3 %collective-permute-start = (bf16[256,1024]{1,0:T(8,128)(2,1)S(1)}, bf16[256,1024]{1,0:T(8,128)(2,1)S(1)}, u32[]{:S(2)}, u32[]{:S(2)}) collective-permute-start(bf16[256,1024]{1,0:T(8,128)(2,1)S(1)} %bitcast.14), channel_id=1, source_target_pairs={{0,8},{1,9},{2,10},{3,11},{4,12},{5,13},{6,14},{7,15},{8,16},{9,17... | collective-permute-start | bytes 1572872 | tf_op jit(solution)/shard_map/ppermute | solution.py:471
  31.0 13.0 %collective-permute-start.1 = (bf16[256,1024]{1,0:T(8,128)(2,1)S(1)}, bf16[256,1024]{1,0:T(8,128)(2,1)S(1)}, u32[]{:S(2)}, u32[]{:S(2)}) collective-permute-start(bf16[256,1024]{1,0:T(8,128)(2,1)S(1)} %bitcast.15), channel_id=1, source_target_pairs={{0,24},{1,25},{2,26},{3,27},{4,28},{5,29},{6,30},{7,31},{8,0},{9,1... | collective-permute-start | bytes 1572872 | tf_op jit(solution)/shard_map/ppermute | solution.py:471
  44.0 15.4 %collective-permute-start.9 = (bf16[256,1024]{1,0:T(8,128)(2,1)S(1)}, bf16[256,1024]{1,0:T(8,128)(2,1)S(1)}, u32[]{:S(2)}, u32[]{:S(2)}) collective-permute-start(bf16[256,1024]{1,0:T(8,128)(2,1)S(1)} %collective-permute-done.refs_1_), channel_id=1, source_target_pairs={{0,8},{1,9},{2,10},{3,11},{4,12},{5,13},{6,14},{7,15},{8,16},{9,17... | collective-permute-start | bytes 1572872 | tf_op jit(solution)/shard_map/ppermute | solution.py:474
  45.0 7.6 %collective-permute-start.2 = (bf16[64,1152]{1,0:T(8,128)(2,1)}, bf16[64,1152]{1,0:T(8,128)(2,1)S(1)}, u32[]{:S(2)}, u32[]{:S(2)}) collective-permute-start(bf16[64,1152]{1,0:T(8,128)(2,1)} %predict.3.refs_0_), channel_id=1, source_target_pairs={{0,64},{32,96},{64,128},{96,160},{128,192},{160,224},{192,0},{224,... | collective-permute-start | bytes 442376 | tf_op jit(solution)/shard_map/ppermute | solution.py:478
  46.2 8.9 %collective-permute-start.3 = (bf16[64,1152]{1,0:T(8,128)(2,1)}, bf16[64,1152]{1,0:T(8,128)(2,1)S(1)}, u32[]{:S(2)}, u32[]{:S(2)}) collective-permute-start(bf16[64,1152]{1,0:T(8,128)(2,1)} %predict.3.refs_0_), channel_id=1, source_target_pairs={{0,128},{32,160},{64,192},{96,224},{128,0},{160,32},{192,64},{224,... | collective-permute-start | bytes 442376 | tf_op jit(solution)/shard_map/ppermute | solution.py:478
  48.6 8.2 %collective-permute-start.4 = (bf16[64,1152]{1,0:T(8,128)(2,1)}, bf16[64,1152]{1,0:T(8,128)(2,1)S(1)}, u32[]{:S(2)}, u32[]{:S(2)}) collective-permute-start(bf16[64,1152]{1,0:T(8,128)(2,1)} %predict.3.refs_0_), channel_id=1, source_target_pairs={{0,192},{32,224},{64,0},{96,32},{128,64},{160,96},{192,128},{224,1... | collective-permute-start | bytes 442376 | tf_op jit(solution)/shard_map/ppermute | solution.py:478
  49.8 7.0 %collective-permute-start.5 = (bf16[64,1152]{1,0:T(8,128)(2,1)}, bf16[64,1152]{1,0:T(8,128)(2,1)S(1)}, u32[]{:S(2)}, u32[]{:S(2)}) collective-permute-start(bf16[64,1152]{1,0:T(8,128)(2,1)} %predict.3.refs_0_), channel_id=1, source_target_pairs={{0,32},{32,0},{64,96},{96,64},{128,160},{160,128},{192,224},{224,1... | collective-permute-start | bytes 442376 | tf_op jit(solution)/shard_map/ppermute | solution.py:481
  52.6 4.2 %collective-permute-start.6 = (bf16[64,1152]{1,0:T(8,128)(2,1)S(1)}, bf16[64,1152]{1,0:T(8,128)(2,1)S(1)}, u32[]{:S(2)}, u32[]{:S(2)}) collective-permute-start(bf16[64,1152]{1,0:T(8,128)(2,1)S(1)} %collective-permute-done.2.refs_1_), channel_id=1, source_target_pairs={{0,32},{32,0},{64,96},{96,64},{128,160},{160,128},{192,224},{224,1... | collective-permute-start | bytes 442376 | tf_op jit(solution)/shard_map/ppermute | solution.py:481
  55.1 2.7 %collective-permute-start.7 = (bf16[64,1152]{1,0:T(8,128)(2,1)S(1)}, bf16[64,1152]{1,0:T(8,128)(2,1)S(1)}, u32[]{:S(2)}, u32[]{:S(2)}) collective-permute-start(bf16[64,1152]{1,0:T(8,128)(2,1)S(1)} %collective-permute-done.3.refs_2_), channel_id=1, source_target_pairs={{0,32},{32,0},{64,96},{96,64},{128,160},{160,128},{192,224},{224,1... | collective-permute-start | bytes 442376 | tf_op jit(solution)/shard_map/ppermute | solution.py:481
  56.8 1.4 %collective-permute-start.8 = (bf16[64,1152]{1,0:T(8,128)(2,1)S(1)}, bf16[64,1152]{1,0:T(8,128)(2,1)S(1)}, u32[]{:S(2)}, u32[]{:S(2)}) collective-permute-start(bf16[64,1152]{1,0:T(8,128)(2,1)S(1)} %collective-permute-done.4.refs_3_), channel_id=1, source_target_pairs={{0,32},{32,0},{64,96},{96,64},{128,160},{160,128},{192,224},{224,1... | collective-permute-start | bytes 442376 | tf_op jit(solution)/shard_map/ppermute | solution.py:481
  58.2 0.9 %copy-start = (bf16[64,1152]{1,0:T(8,128)(2,1)S(1)}, bf16[64,1152]{1,0:T(8,128)(2,1)}, u32[]{:S(2)}) copy-start(bf16[64,1152]{1,0:T(8,128)(2,1)} %predict.3.refs_0_) | copy-start | bytes 442372
where the time goes:
time: 76.7 us; the launch traced here: 76.2 us
  Pallas kernels  29.5 us (38%)
  starting transfers between devices  24.5 us (32%)
  blocking collectives  12.8 us (17%)
  waiting for transfers between devices  7.78 us (10%)
  local copies, waits for them, and re-layouts  0.91 us (1%)
    pallas_call x2, Pallas kernels, predict_rows(): pl.pallas_call(functools.partial(predict_kernel, part * peps), grid_spec=...  23.1 us
    all_to_all x1, blocking collectives, local(): lax.all_to_all(pieces, 'seq', split_axis=0, concat_axis=0, tiled=True)  12.8 us
    all_to_all x1, starting transfers between devices, local(): lax.all_to_all(queries, 'seq', split_axis=0, concat_axis=0, tiled=True, a...  9.03 us
    ppermute x4, starting transfers between devices, local(): held = held + [lax.ppermute(part, 'mass', swap) for part in held]  7.01 us
    all_to_all x1, waiting for transfers between devices, local(): lax.all_to_all(queries, 'seq', split_axis=0, concat_axis=0, tiled=True, a...  6.39 us
    ppermute x3, starting transfers between devices, local(): lax.ppermute(rows, 'mass', [(i, (i + d) % masses) for i in range(masses)])  4.82 us
    pallas_call x1, Pallas kernels, score(): pl.pallas_call(functools.partial(score_kernel, zs), in_specs=[pl.BlockSpe...  2.5 us
    pallas_call x1, Pallas kernels, prepare_queries(): pl.pallas_call(functools.partial(query_kernel, copies), out_shape=jax.Sha...  2.07 us
  transfers between devices with their start and end apart: 11, of which 3 were waited for; matrix products, arithmetic and copies ran while one was open for 0% of the time, Pallas kernels for 31%

commit v1 on v0

--- a/solution.py
+++ b/solution.py
@@ -26,6 +26,8 @@
 TILE = 128
 GROUP = 8
 PIECES = 1
+SHARES = 2
+LAG = 0
 ROWW = SPEC + 128
 VMEM_LIMIT = 60 * 1024 * 1024
 NT = (((1,), (1,)), ((), ()))
@@ -67,6 +69,7 @@
         up = jnp.dot(normed, w_up_ref[:, c : c + D], preferred_element_type=F32)
         hidden = gelu(up).astype(BF)
         state = state + jnp.dot(hidden, w_down_ref[c : c + D, :], preferred_element_type=F32)
+        yield
     return state
 
 
@@ -85,6 +88,7 @@
         ]
         spread = jnp.concatenate(spread, axis=0)
         scores.append(jnp.dot(key, spread, preferred_element_type=F32))
+    yield
     wide = []
     for score, (_, _, _, length) in zip(scores, items):
         own = score[:L]
@@ -102,6 +106,7 @@
                 [jnp.where(lane == j, probs, jnp.zeros_like(probs)) for j in range(peps)], axis=0
             )
         )
+    yield
     heard = []
     for probs, (_, _, value, _) in zip(wide, items):
         turned = value.T
@@ -118,7 +123,53 @@
                 axis=0,
             )
         )
+    yield
     return [out.T.astype(BF) for out in heard]
+
+
+def transform(state, tile_lengths, refs, waits):
+    w_qkv_ref, w_out_ref, w_up_ref, w_down_ref, gain_ref = refs
+    for layer in range(NL):
+        normed = norm_rows(state, gain_ref[layer, 0:1, :].astype(F32))
+        waits(layer)
+        mixed = [
+            jnp.dot(
+                normed, w_qkv_ref[layer, :, c * D : (c + 1) * D], preferred_element_type=F32
+            ).astype(BF)
+            for c in range(3)
+        ]
+        yield
+        items = [
+            [m[t * TILE : (t + 1) * TILE, g * TILE : (g + 1) * TILE] for m in mixed] + [tile_lengths[t]]
+            for t in range(state.shape[0] // TILE)
+            for g in range(D // TILE)
+        ]
+        heard = []
+        for i in range(0, len(items), GROUP):
+            heard = heard + (yield from attend(items[i : i + GROUP]))
+        attended = jnp.concatenate(
+            [jnp.concatenate(heard[i : i + 2], axis=1) for i in range(0, len(heard), 2)], axis=0
+        )
+        state = state + jnp.dot(attended, w_out_ref[layer], preferred_element_type=F32)
+        normed = norm_rows(state, gain_ref[layer, 1:2, :].astype(F32))
+        yield
+        state = yield from feed_forward(state, normed, w_up_ref.at[layer], w_down_ref.at[layer])
+    return state
+
+
+def interleave(shares):
+    results, step = [None] * len(shares), 0
+    running = list(range(len(shares)))
+    while running:
+        for i in list(running):
+            if step >= i * LAG:
+                try:
+                    next(shares[i])
+                except StopIteration as stop:
+                    results[i] = stop.value
+                    running.remove(i)
+        step += 1
+    return results
 
 
 def predict_kernel(
@@ -179,30 +230,28 @@
             vec = jnp.where(lane == j, lengths_ref[first + t * 4 + j], vec)
         tile_lengths.append(vec)
 
-    for layer in range(NL):
-        normed = norm_rows(state, gain_ref[layer, 0:1, :].astype(F32))
-        for move in moves[layer]:
-            move.wait()
-        mixed = [
-            jnp.dot(
-                normed, w_qkv_ref[layer, :, c * D : (c + 1) * D], preferred_element_type=F32
-            ).astype(BF)
-            for c in range(3)
+    seen = set()
+
+    def waits(layer):
+        if layer not in seen:
+            seen.add(layer)
+            for move in moves[layer]:
+                move.wait()
+
+    share = STEP // SHARES
+    refs = (w_qkv_ref, w_out_ref, w_up_ref, w_down_ref, gain_ref)
+    state = interleave(
+        [
+            transform(
+                state[i * share : (i + 1) * share],
+                tile_lengths[i * share // TILE : (i + 1) * share // TILE],
+                refs,
+                waits,
+            )
+            for i in range(SHARES)
         ]
-        items = [
-            [m[t * TILE : (t + 1) * TILE, g * TILE : (g + 1) * TILE] for m in mixed] + [tile_lengths[t]]
-            for t in range(STEP // TILE)
-            for g in range(D // TILE)
-        ]
-        heard = []
-        for i in range(0, len(items), GROUP):
-            heard = heard + attend(items[i : i + GROUP])
-        attended = jnp.concatenate(
-            [jnp.concatenate(heard[i : i + 2], axis=1) for i in range(0, len(heard), 2)], axis=0
-        )
-        state = state + jnp.dot(attended, w_out_ref[layer], preferred_element_type=F32)
-        normed = norm_rows(state, gain_ref[layer, 1:2, :].astype(F32))
-        state = feed_forward(state, normed, w_up_ref.at[layer], w_down_ref.at[layer])
+    )
+    state = jnp.concatenate(state, axis=0)
     normed = norm_rows(state, final_ref[...].reshape(1, D).astype(F32))
     head = jnp.concatenate([w_head_ref[...]] * 4, axis=0)
     logit_ref[...] = lax.dot_general(normed, head, NT, preferred_element_type=F32)
@@ -278,9 +327,9 @@
         operands += (before,)
         in_specs += [pl.BlockSpec(memory_space=pl.ANY)]
     grid = pltpu.PrefetchScalarGridSpec(
-        num_scalar_prefetch=len(scalars),
+        num_scalar_prefetch=0,
         grid=(1,),
-        in_specs=in_specs,
+        in_specs=[pl.BlockSpec(memory_space=pltpu.SMEM)] * len(scalars) + in_specs,
         out_specs=pl.BlockSpec((peps, ROWW), lambda i, *_: (part, 0)),
         scratch_shapes=[pltpu.VMEM((STEP, 128), F32)]
         + [pltpu.VMEM(weight.shape, BF) for weight in large]

time: 76.7 us -> 76.7 us (level)
  Pallas kernels: 29.5 us -> 27.5 us
  waiting for transfers between devices: 7.78 us -> 9.78 us
    pallas_call x2, Pallas kernels: 23.1 us -> 21.1 us  [predict_rows(): pl.pallas_call(functools.partial(predict_kernel, part * peps), grid_spec=...]
    ppermute x1, waiting for transfers between devices: 0.02 us -> 1.02 us  [local(): lax.ppermute(queries, 'seq', ahead)]
    all_to_all x1, waiting for transfers between devices: 6.39 us -> 7.39 us  [local(): lax.all_to_all(queries, 'seq', split_axis=0, concat_axis=0, tiled=True, a...]
  transfers between devices with their start and end apart: 11 -> 11, of which waited for: 3 -> 4; matrix products, arithmetic and copies ran while one was open for 0% -> 0% of each run, Pallas kernels for 31% -> 28%
where the time goes in v1:
time: 76.7 us; the launch traced here: 76.2 us
  Pallas kernels  27.5 us (36%)
  starting transfers between devices  24.5 us (32%)
  blocking collectives  12.8 us (17%)
  waiting for transfers between devices  9.78 us (13%)
  local copies, waits for them, and re-layouts  0.91 us (1%)
    pallas_call x2, Pallas kernels, predict_rows(): pl.pallas_call(functools.partial(predict_kernel, part * peps), grid_spec=...  21.1 us
    all_to_all x1, blocking collectives, local(): lax.all_to_all(pieces, 'seq', split_axis=0, concat_axis=0, tiled=True)  12.8 us
    all_to_all x1, starting transfers between devices, local(): lax.all_to_all(queries, 'seq', split_axis=0, concat_axis=0, tiled=True, a...  9.03 us
    all_to_all x1, waiting for transfers between devices, local(): lax.all_to_all(queries, 'seq', split_axis=0, concat_axis=0, tiled=True, a...  7.39 us
    ppermute x4, starting transfers between devices, local(): held = held + [lax.ppermute(part, 'mass', swap) for part in held]  7.01 us
    ppermute x3, starting transfers between devices, local(): lax.ppermute(rows, 'mass', [(i, (i + d) % masses) for i in range(masses)])  4.82 us
    pallas_call x1, Pallas kernels, score(): pl.pallas_call(functools.partial(score_kernel, zs), in_specs=[pl.BlockSpe...  2.5 us
    pallas_call x1, Pallas kernels, prepare_queries(): pl.pallas_call(functools.partial(query_kernel, copies), out_shape=jax.Sha...  2.07 us
  transfers between devices with their start and end apart: 11, of which 4 were waited for; matrix products, arithmetic and copies ran while one was open for 0% of the time, Pallas kernels for 28%

profile of v1, /device:TPU:1, one launch (start us, length us, event | category | flops | bytes accessed | tf_op | source)
XLA Modules:
  0.0 76.2 jit_solution(3519504955050921360)
XLA Ops:
  0.6 2.1 %prepare.1 = bf16[8,32,1024]{2,1,0:T(8,128)(2,1)} custom-call(s32[1,32]{1,0:T(1,128)} %bitcast.19, bf16[32,1024]{1,0:T(8,128)(2,1)} %spectra_ref.1), custom_call_target="tpu_custom_call" | custom-call | tf_op jit(solution)/shard_map/prepare/pallas_call | solution.py:378
  2.7 9.0 %all-to-all-start = ((bf16[8,32,1024]{2,1,0:T(8,128)(2,1)}), bf16[8,32,1024]{2,1,0:T(8,128)(2,1)S(1)}, u32[]{:S(2)}, u32[]{:S(2)}) async-start(bf16[8,32,1024]{2,1,0:T(8,128)(2,1)} %prepare.1), calls=%async_computation | async-start | bytes 1048576 | tf_op jit(solution)/shard_map/all_to_all | solution.py:514
  11.7 10.6 %predict.2.refs_0_ = bf16[64,1152]{1,0:T(8,128)(2,1)} custom-call(s32[64]{0:T(128)} %lengths_ref.2, s32[64]{0:T(128)} %bitcast.25, s32[64]{0:T(128)} %tsub_ref.3, s32[64]{0:T(128)} %bitcast.27, s32[64]{0:T(128)} %dsub_ref.3, s32[32,64]{1,0:T(8,128)} %bitcast.21, bf16[32,256]{1,0:T(8,128)(2,1)} %embedding_ref.3, f32[32,256]{1,0:T(8,128)} %constant.11.clone.code_ref, ...), custom_call_target="tpu_custom_call" | custom-call | flops 3221225472 | bytes 4194304 | tf_op jit(solution)/shard_map/predict/pallas_call | solution.py:339
  22.3 7.4 %all-to-all-done = bf16[8,32,1024]{2,1,0:T(8,128)(2,1)S(1)} async-done(((bf16[8,32,1024]{2,1,0:T(8,128)(2,1)}), bf16[8,32,1024]{2,1,0:T(8,128)(2,1)S(1)}, u32[]{:S(2)}, u32[]{:S(2)}) %all-to-all-start) | async-done | bytes 524320 | tf_op jit(solution)/shard_map/all_to_all | solution.py:514
  29.7 1.3 %collective-permute-start = (bf16[256,1024]{1,0:T(8,128)(2,1)S(1)}, bf16[256,1024]{1,0:T(8,128)(2,1)S(1)}, u32[]{:S(2)}, u32[]{:S(2)}) collective-permute-start(bf16[256,1024]{1,0:T(8,128)(2,1)S(1)} %bitcast.14), channel_id=1, source_target_pairs={{0,8},{1,9},{2,10},{3,11},{4,12},{5,13},{6,14},{7,15},{8,16},{9,17... | collective-permute-start | bytes 1572872 | tf_op jit(solution)/shard_map/ppermute | solution.py:520
  31.0 1.4 %collective-permute-start.1 = (bf16[256,1024]{1,0:T(8,128)(2,1)S(1)}, bf16[256,1024]{1,0:T(8,128)(2,1)S(1)}, u32[]{:S(2)}, u32[]{:S(2)}) collective-permute-start(bf16[256,1024]{1,0:T(8,128)(2,1)S(1)} %bitcast.15), channel_id=1, source_target_pairs={{0,24},{1,25},{2,26},{3,27},{4,28},{5,29},{6,30},{7,31},{8,0},{9,1... | collective-permute-start | bytes 1572872 | tf_op jit(solution)/shard_map/ppermute | solution.py:520
  32.4 10.6 %predict.3.refs_0_ = bf16[64,1152]{1,0:T(8,128)(2,1)} custom-call(s32[64]{0:T(128)} %lengths_ref.2, s32[64]{0:T(128)} %bitcast.26, s32[64]{0:T(128)} %tsub_ref.3, s32[64]{0:T(128)} %bitcast.28, s32[64]{0:T(128)} %dsub_ref.3, s32[32,64]{1,0:T(8,128)} %bitcast.22, bf16[32,256]{1,0:T(8,128)(2,1)} %embedding_ref.3, ...), custom_call_target="tpu_custom_call", output_to_operand_aliasing={{}: (15, {})} | custom-call | flops 3221225472 | bytes 4194304 | tf_op jit(solution)/shard_map/predict/pallas_call | solution.py:339
  43.0 1.0 %collective-permute-done.refs_1_ = bf16[256,1024]{1,0:T(8,128)(2,1)S(1)} collective-permute-done((bf16[256,1024]{1,0:T(8,128)(2,1)S(1)}, bf16[256,1024]{1,0:T(8,128)(2,1)S(1)}, u32[]{:S(2)}, u32[]{:S(2)}) %collective-permute-start) | collective-permute-done | bytes 524320 | tf_op jit(solution)/shard_map/ppermute | solution.py:520
  44.0 0.0 collective-permute-done.1.refs_3_
  44.0 0.9 %collective-permute-start.9 = (bf16[256,1024]{1,0:T(8,128)(2,1)S(1)}, bf16[256,1024]{1,0:T(8,128)(2,1)S(1)}, u32[]{:S(2)}, u32[]{:S(2)}) collective-permute-start(bf16[256,1024]{1,0:T(8,128)(2,1)S(1)} %collective-permute-done.refs_1_), channel_id=1, source_target_pairs={{0,8},{1,9},{2,10},{3,11},{4,12},{5,13},{6,14},{7,15},{8,16},{9,17... | collective-permute-start | bytes 1572872 | tf_op jit(solution)/shard_map/ppermute | solution.py:523
  45.0 1.2 %collective-permute-start.2 = (bf16[64,1152]{1,0:T(8,128)(2,1)}, bf16[64,1152]{1,0:T(8,128)(2,1)S(1)}, u32[]{:S(2)}, u32[]{:S(2)}) collective-permute-start(bf16[64,1152]{1,0:T(8,128)(2,1)} %predict.3.refs_0_), channel_id=1, source_target_pairs={{0,64},{32,96},{64,128},{96,160},{128,192},{160,224},{192,0},{224,... | collective-permute-start | bytes 442376 | tf_op jit(solution)/shard_map/ppermute | solution.py:527
  46.2 2.4 %collective-permute-start.3 = (bf16[64,1152]{1,0:T(8,128)(2,1)}, bf16[64,1152]{1,0:T(8,128)(2,1)S(1)}, u32[]{:S(2)}, u32[]{:S(2)}) collective-permute-start(bf16[64,1152]{1,0:T(8,128)(2,1)} %predict.3.refs_0_), channel_id=1, source_target_pairs={{0,128},{32,160},{64,192},{96,224},{128,0},{160,32},{192,64},{224,... | collective-permute-start | bytes 442376 | tf_op jit(solution)/shard_map/ppermute | solution.py:527
  48.6 1.2 %collective-permute-start.4 = (bf16[64,1152]{1,0:T(8,128)(2,1)}, bf16[64,1152]{1,0:T(8,128)(2,1)S(1)}, u32[]{:S(2)}, u32[]{:S(2)}) collective-permute-start(bf16[64,1152]{1,0:T(8,128)(2,1)} %predict.3.refs_0_), channel_id=1, source_target_pairs={{0,192},{32,224},{64,0},{96,32},{128,64},{160,96},{192,128},{224,1... | collective-permute-start | bytes 442376 | tf_op jit(solution)/shard_map/ppermute | solution.py:527
  49.8 2.8 %collective-permute-start.5 = (bf16[64,1152]{1,0:T(8,128)(2,1)}, bf16[64,1152]{1,0:T(8,128)(2,1)S(1)}, u32[]{:S(2)}, u32[]{:S(2)}) collective-permute-start(bf16[64,1152]{1,0:T(8,128)(2,1)} %predict.3.refs_0_), channel_id=1, source_target_pairs={{0,32},{32,0},{64,96},{96,64},{128,160},{160,128},{192,224},{224,1... | collective-permute-start | bytes 442376 | tf_op jit(solution)/shard_map/ppermute | solution.py:530
  52.6 0.0 collective-permute-done.2.refs_1_
  52.6 2.5 %collective-permute-start.6 = (bf16[64,1152]{1,0:T(8,128)(2,1)S(1)}, bf16[64,1152]{1,0:T(8,128)(2,1)S(1)}, u32[]{:S(2)}, u32[]{:S(2)}) collective-permute-start(bf16[64,1152]{1,0:T(8,128)(2,1)S(1)} %collective-permute-done.2.refs_1_), channel_id=1, source_target_pairs={{0,32},{32,0},{64,96},{96,64},{128,160},{160,128},{192,224},{224,1... | collective-permute-start | bytes 442376 | tf_op jit(solution)/shard_map/ppermute | solution.py:530
  55.0 0.0 collective-permute-done.3.refs_2_
  55.0 1.7 %collective-permute-start.7 = (bf16[64,1152]{1,0:T(8,128)(2,1)S(1)}, bf16[64,1152]{1,0:T(8,128)(2,1)S(1)}, u32[]{:S(2)}, u32[]{:S(2)}) collective-permute-start(bf16[64,1152]{1,0:T(8,128)(2,1)S(1)} %collective-permute-done.3.refs_2_), channel_id=1, source_target_pairs={{0,32},{32,0},{64,96},{96,64},{128,160},{160,128},{192,224},{224,1... | collective-permute-start | bytes 442376 | tf_op jit(solution)/shard_map/ppermute | solution.py:530
  56.8 0.0 collective-permute-done.4.refs_3_
  56.8 0.0 collective-permute-start.8
  56.8 0.0 collective-permute-done.5.refs_4_
  56.8 0.0 collective-permute-done.6.refs_5_
  56.8 1.0 %collective-permute-done.7.refs_6_ = bf16[64,1152]{1,0:T(8,128)(2,1)S(1)} collective-permute-done((bf16[64,1152]{1,0:T(8,128)(2,1)S(1)}, bf16[64,1152]{1,0:T(8,128)(2,1)S(1)}, u32[]{:S(2)}, u32[]{:S(2)}) %collective-permute-start.7) | collective-permute-done | bytes 147488 | tf_op jit(solution)/shard_map/ppermute | solution.py:530
  57.8 0.4 collective-permute-done.8.refs_7_
  58.2 0.0 copy-start
  58.2 0.9 %copy-done = bf16[64,1152]{1,0:T(8,128)(2,1)S(1)} copy-done((bf16[64,1152]{1,0:T(8,128)(2,1)S(1)}, bf16[64,1152]{1,0:T(8,128)(2,1)}, u32[]{:S(2)}) %copy-start) | copy-done | bytes 147480
  59.1 0.4 turn.1
  59.5 0.0 collective-permute-done.9.refs_2_
  59.5 2.5 %score.1 = f32[32,128]{1,0:T(8,128)S(1)} custom-call(s32[1]{0:T(128)} %bitcast.1.seq_ref, bf16[1024,1024]{1,0:T(8,128)(2,1)S(1)} %get-tuple-element.16.side_ref, f32[8,1024]{1,0:T(8,128)S(1)} %get-tuple-element.17.subs_ref, bf16[256,1024]{1,0:T(8,128)(2,1)S(1)} %bitcast.16, bf16[256,1024]{1,0:T(8,128)(2,1)S(1)} %collective-permute-done.refs_1_, ...), custom_call_target="tpu_custom_call" | custom-call | tf_op jit(solution)/shard_map/score/pallas_call | solution.py:461
  62.0 12.8 %all_to_all.10 = f32[32,1,128]{2,1,0:T(1,128)} all-to-all(f32[32,1,128]{2,1,0:T(1,128)S(1)} %bitcast.17), channel_id=1, replica_groups=mesh['mass'=8,'seq'=32] {'seq'}, dimensions={0} | all-to-all | bytes 32768 | tf_op jit(solution)/shard_map/all_to_all | solution.py:534
  74.8 1.4 %finish.1 = (f32[1,32]{1,0:T(1,128)}, f32[1,32]{1,0:T(1,128)}) custom-call(s32[1,32]{1,0:T(1,128)} %bitcast.20, f32[32,128]{1,0:T(8,128)} %bitcast.18), custom_call_target="tpu_custom_call" | custom-call | tf_op jit(solution)/shard_map/finish/pallas_call | solution.py:484
Async XLA Ops:
  2.7 27.0 %all-to-all-start = ((bf16[8,32,1024]{2,1,0:T(8,128)(2,1)}), bf16[8,32,1024]{2,1,0:T(8,128)(2,1)S(1)}, u32[]{:S(2)}, u32[]{:S(2)}) async-start(bf16[8,32,1024]{2,1,0:T(8,128)(2,1)} %prepare.1), calls=%async_computation | async-start | bytes 1048576 | tf_op jit(solution)/shard_map/all_to_all | solution.py:514
  29.7 14.3 %collective-permute-start = (bf16[256,1024]{1,0:T(8,128)(2,1)S(1)}, bf16[256,1024]{1,0:T(8,128)(2,1)S(1)}, u32[]{:S(2)}, u32[]{:S(2)}) collective-permute-start(bf16[256,1024]{1,0:T(8,128)(2,1)S(1)} %bitcast.14), channel_id=1, source_target_pairs={{0,8},{1,9},{2,10},{3,11},{4,12},{5,13},{6,14},{7,15},{8,16},{9,17... | collective-permute-start | bytes 1572872 | tf_op jit(solution)/shard_map/ppermute | solution.py:520
  31.0 13.0 %collective-permute-start.1 = (bf16[256,1024]{1,0:T(8,128)(2,1)S(1)}, bf16[256,1024]{1,0:T(8,128)(2,1)S(1)}, u32[]{:S(2)}, u32[]{:S(2)}) collective-permute-start(bf16[256,1024]{1,0:T(8,128)(2,1)S(1)} %bitcast.15), channel_id=1, source_target_pairs={{0,24},{1,25},{2,26},{3,27},{4,28},{5,29},{6,30},{7,31},{8,0},{9,1... | collective-permute-start | bytes 1572872 | tf_op jit(solution)/shard_map/ppermute | solution.py:520
  44.0 15.4 %collective-permute-start.9 = (bf16[256,1024]{1,0:T(8,128)(2,1)S(1)}, bf16[256,1024]{1,0:T(8,128)(2,1)S(1)}, u32[]{:S(2)}, u32[]{:S(2)}) collective-permute-start(bf16[256,1024]{1,0:T(8,128)(2,1)S(1)} %collective-permute-done.refs_1_), channel_id=1, source_target_pairs={{0,8},{1,9},{2,10},{3,11},{4,12},{5,13},{6,14},{7,15},{8,16},{9,17... | collective-permute-start | bytes 1572872 | tf_op jit(solution)/shard_map/ppermute | solution.py:523
  45.0 7.6 %collective-permute-start.2 = (bf16[64,1152]{1,0:T(8,128)(2,1)}, bf16[64,1152]{1,0:T(8,128)(2,1)S(1)}, u32[]{:S(2)}, u32[]{:S(2)}) collective-permute-start(bf16[64,1152]{1,0:T(8,128)(2,1)} %predict.3.refs_0_), channel_id=1, source_target_pairs={{0,64},{32,96},{64,128},{96,160},{128,192},{160,224},{192,0},{224,... | collective-permute-start | bytes 442376 | tf_op jit(solution)/shard_map/ppermute | solution.py:527
  46.2 8.9 %collective-permute-start.3 = (bf16[64,1152]{1,0:T(8,128)(2,1)}, bf16[64,1152]{1,0:T(8,128)(2,1)S(1)}, u32[]{:S(2)}, u32[]{:S(2)}) collective-permute-start(bf16[64,1152]{1,0:T(8,128)(2,1)} %predict.3.refs_0_), channel_id=1, source_target_pairs={{0,128},{32,160},{64,192},{96,224},{128,0},{160,32},{192,64},{224,... | collective-permute-start | bytes 442376 | tf_op jit(solution)/shard_map/ppermute | solution.py:527
  48.6 8.2 %collective-permute-start.4 = (bf16[64,1152]{1,0:T(8,128)(2,1)}, bf16[64,1152]{1,0:T(8,128)(2,1)S(1)}, u32[]{:S(2)}, u32[]{:S(2)}) collective-permute-start(bf16[64,1152]{1,0:T(8,128)(2,1)} %predict.3.refs_0_), channel_id=1, source_target_pairs={{0,192},{32,224},{64,0},{96,32},{128,64},{160,96},{192,128},{224,1... | collective-permute-start | bytes 442376 | tf_op jit(solution)/shard_map/ppermute | solution.py:527
  49.8 7.0 %collective-permute-start.5 = (bf16[64,1152]{1,0:T(8,128)(2,1)}, bf16[64,1152]{1,0:T(8,128)(2,1)S(1)}, u32[]{:S(2)}, u32[]{:S(2)}) collective-permute-start(bf16[64,1152]{1,0:T(8,128)(2,1)} %predict.3.refs_0_), channel_id=1, source_target_pairs={{0,32},{32,0},{64,96},{96,64},{128,160},{160,128},{192,224},{224,1... | collective-permute-start | bytes 442376 | tf_op jit(solution)/shard_map/ppermute | solution.py:530
  52.6 4.2 %collective-permute-start.6 = (bf16[64,1152]{1,0:T(8,128)(2,1)S(1)}, bf16[64,1152]{1,0:T(8,128)(2,1)S(1)}, u32[]{:S(2)}, u32[]{:S(2)}) collective-permute-start(bf16[64,1152]{1,0:T(8,128)(2,1)S(1)} %collective-permute-done.2.refs_1_), channel_id=1, source_target_pairs={{0,32},{32,0},{64,96},{96,64},{128,160},{160,128},{192,224},{224,1... | collective-permute-start | bytes 442376 | tf_op jit(solution)/shard_map/ppermute | solution.py:530
  55.0 2.7 %collective-permute-start.7 = (bf16[64,1152]{1,0:T(8,128)(2,1)S(1)}, bf16[64,1152]{1,0:T(8,128)(2,1)S(1)}, u32[]{:S(2)}, u32[]{:S(2)}) collective-permute-start(bf16[64,1152]{1,0:T(8,128)(2,1)S(1)} %collective-permute-done.3.refs_2_), channel_id=1, source_target_pairs={{0,32},{32,0},{64,96},{96,64},{128,160},{160,128},{192,224},{224,1... | collective-permute-start | bytes 442376 | tf_op jit(solution)/shard_map/ppermute | solution.py:530
  56.8 1.4 %collective-permute-start.8 = (bf16[64,1152]{1,0:T(8,128)(2,1)S(1)}, bf16[64,1152]{1,0:T(8,128)(2,1)S(1)}, u32[]{:S(2)}, u32[]{:S(2)}) collective-permute-start(bf16[64,1152]{1,0:T(8,128)(2,1)S(1)} %collective-permute-done.4.refs_3_), channel_id=1, source_target_pairs={{0,32},{32,0},{64,96},{96,64},{128,160},{160,128},{192,224},{224,1... | collective-permute-start | bytes 442376 | tf_op jit(solution)/shard_map/ppermute | solution.py:530
  58.2 0.9 %copy-start = (bf16[64,1152]{1,0:T(8,128)(2,1)S(1)}, bf16[64,1152]{1,0:T(8,128)(2,1)}, u32[]{:S(2)}) copy-start(bf16[64,1152]{1,0:T(8,128)(2,1)} %predict.3.refs_0_) | copy-start | bytes 442372

commit v2 on v1

--- a/solution.py
+++ b/solution.py
@@ -28,7 +28,7 @@
 PIECES = 1
 SHARES = 2
 LAG = 0
-ROWW = SPEC + 128
+LAST = SPEC - ION
 VMEM_LIMIT = 60 * 1024 * 1024
 NT = (((1,), (1,)), ((), ()))
 
@@ -272,12 +272,17 @@
     for i in range(peps):
         length = jnp.where(row == i, lengths_ref[first + i], length)
         for c, ref in enumerate((towner_ref, tsub_ref, downer_ref, dsub_ref)):
-            tag = jnp.where((row == i) & (column == c), ref[first + i], tag)
+            tag = jnp.where((row == i) & (column == LAST % 128 + 1 + c), ref[first + i], tag)
     position = lane_iota((peps, SPEC)) // ION
     length = jnp.concatenate([length] * (SPEC // 128), axis=1)
     intensity = jnp.where(position < length - 1, intensity, F32(0.0))
-    rows_ref[:, :SPEC] = standardize(intensity)
-    rows_ref[:, SPEC:] = tag.astype(F32).astype(BF)
+    spectra = standardize(intensity)
+    rows_ref[:, : SPEC - 128] = spectra[:, : SPEC - 128]
+    rows_ref[:, SPEC - 128 :] = jnp.where(
+        (column > LAST % 128) & (column <= LAST % 128 + 4),
+        tag.astype(F32).astype(BF),
+        spectra[:, SPEC - 128 :],
+    )
 
 
 def predict_rows(
@@ -330,7 +335,7 @@
         num_scalar_prefetch=0,
         grid=(1,),
         in_specs=[pl.BlockSpec(memory_space=pltpu.SMEM)] * len(scalars) + in_specs,
-        out_specs=pl.BlockSpec((peps, ROWW), lambda i, *_: (part, 0)),
+        out_specs=pl.BlockSpec((peps, SPEC), lambda i, *_: (part, 0)),
         scratch_shapes=[pltpu.VMEM((STEP, 128), F32)]
         + [pltpu.VMEM(weight.shape, BF) for weight in large]
         + [pltpu.SemaphoreType.DMA((NL, len(large), PIECES))],
@@ -339,7 +344,7 @@
     return pl.pallas_call(
         functools.partial(predict_kernel, part * peps),
         grid_spec=grid,
-        out_shape=jax.ShapeDtypeStruct((count, ROWW), BF),
+        out_shape=jax.ShapeDtypeStruct((count, SPEC), BF),
         input_output_aliases=aliases,
         compiler_params=pltpu.CompilerParams(vmem_limit_bytes=VMEM_LIMIT),
         cost_estimate=pl.CostEstimate(
@@ -387,24 +392,23 @@
 
 def turn_kernel(mass_ref, *refs):
     sources, (side_ref, subs_ref) = refs[:-2], refs[-2:]
-    count = sources[0].shape[0]
-    per = 128 // count
-    half = len(sources) * count
+    per = 128 // sources[0].shape[0]
+    half = side_ref.shape[1] // 2
     me = mass_ref[0].astype(F32)
     for i in range(len(sources) // per):
-        group = sources[i * per : (i + 1) * per]
-        turned = jnp.concatenate([ref[:, :SPEC] for ref in group], axis=0).T
-        lanes = pl.ds(i * 128, 128)
-        side_ref[:, lanes] = turned
-        for p in range(L):
-            side_ref[p * ION : (p + 1) * ION, pl.ds(half + i * 128, 128)] = turned[
-                (L - 1 - p) * ION : (L - p) * ION
-            ]
-        tags = jnp.concatenate([ref[:, SPEC:] for ref in group], axis=0).astype(F32).T
-        for kind in range(2):
-            owner, sub = tags[2 * kind : 2 * kind + 1], tags[2 * kind + 1 : 2 * kind + 2]
+        turned = jnp.concatenate([ref[...] for ref in sources[i * per : (i + 1) * per]], axis=0).T
+        last = turned[LAST : LAST + 16].astype(F32)
+        background = jnp.broadcast_to(last[:1], (ION, 128)).astype(BF)
+        targets, decoys = pl.ds(i * 128, 128), pl.ds(half + i * 128, 128)
+        side_ref[:LAST, targets] = turned[:LAST]
+        side_ref[LAST:, targets] = background
+        side_ref[:ION, decoys] = background
+        for p in range(1, L):
+            side_ref[p * ION : (p + 1) * ION, decoys] = turned[(L - 1 - p) * ION : (L - p) * ION]
+        for kind, lanes in enumerate((targets, decoys)):
+            owner, sub = last[1 + 2 * kind : 2 + 2 * kind], last[2 + 2 * kind : 3 + 2 * kind]
             sub = jnp.where(owner == me, sub, F32(-1.0))
-            subs_ref[:, pl.ds(kind * half + i * 128, 128)] = jnp.broadcast_to(sub, (8, 128))
+            subs_ref[:, lanes] = jnp.broadcast_to(sub, (8, 128))
 
 
 def turn(mass, sources):
@@ -423,9 +427,8 @@
     )(mass, *sources)
 
 
-def score_kernel(zs, seq_ref, side_ref, subs_ref, *refs):
-    blocks, out_ref = refs[:-1], refs[-1]
-    half = side_ref.shape[1] // 2
+def score_kernel(zs, sides, seq_ref, *refs):
+    turned, blocks, out_ref = refs[: 2 * sides], refs[2 * sides : -1], refs[-1]
     y = lax.div(seq_ref[0], zs)
     low, row = lane_iota((8, 128)) < 32, row_iota((8, 128))
     for back, block in enumerate(blocks):
@@ -433,18 +436,19 @@
         count = queries.shape[0]
         there = lax.rem(y + len(blocks) - back, len(blocks))
         bins = (row_iota((count, 128)) // QPB + there * (count // QPB)).astype(F32)
-        best = []
-        for kind in range(2):
-            scores = jnp.dot(
-                queries, side_ref[:, kind * half : (kind + 1) * half], preferred_element_type=F32
-            )
-            top = jnp.zeros((count, 128), F32)
-            for i in range(half // 128):
-                sub = subs_ref[:1, kind * half + i * 128 : kind * half + (i + 1) * 128]
-                top = jnp.maximum(
-                    top, jnp.where(sub == bins, scores[:, i * 128 : (i + 1) * 128], F32(0.0))
+        tops = [jnp.zeros((count, 128), F32) for _ in range(2)]
+        for side_ref, subs_ref in zip(turned[0::2], turned[1::2]):
+            scores = jnp.dot(queries, side_ref[...], preferred_element_type=F32)
+            tiles = scores.shape[1] // 128
+            for i in range(tiles):
+                kind = 2 * i // tiles
+                own = jnp.where(
+                    subs_ref[:1, i * 128 : (i + 1) * 128] == bins,
+                    scores[:, i * 128 : (i + 1) * 128],
+                    F32(0.0),
                 )
-            best.append(jnp.max(top.T, axis=0, keepdims=True) * F32(1.0 / math.sqrt(SPEC)))
+                tops[kind] = jnp.maximum(tops[kind], own)
+        best = [jnp.max(top.T, axis=0, keepdims=True) * F32(1.0 / math.sqrt(SPEC)) for top in tops]
         out = jnp.zeros((8, 128), F32)
         for z in range(zs):
             tile, shift = z // 4, 32 * (z % 4)
@@ -455,17 +459,17 @@
         out_ref[pl.ds(pl.multiple_of(there * zs, 8), zs), :] = out
 
 
-def score(zs, seq, side, subs, blocks):
+def score(zs, seq, sides, blocks):
     inside = pl.BlockSpec(memory_space=pltpu.VMEM)
     queries = len(blocks) * blocks[0].shape[0]
     return pl.pallas_call(
-        functools.partial(score_kernel, zs),
-        in_specs=[pl.BlockSpec(memory_space=pltpu.SMEM)] + [inside] * (2 + len(blocks)),
+        functools.partial(score_kernel, zs, len(sides)),
+        in_specs=[pl.BlockSpec(memory_space=pltpu.SMEM)] + [inside] * (2 * len(sides) + len(blocks)),
         out_specs=inside,
         out_shape=jax.ShapeDtypeStruct((queries // 32, 128), F32),
         compiler_params=pltpu.CompilerParams(vmem_limit_bytes=32 * 1024 * 1024),
         name="score",
-    )(seq, side, subs, *blocks)
+    )(seq, *[part for side in sides for part in side], *blocks)
 
 
 def finish_kernel(bins_ref, pieces_ref, target_ref, decoy_ref):
@@ -523,14 +527,14 @@
     blocks[2] = lax.ppermute(blocks[1], "seq", ahead)
     masses = lax.axis_size("mass")
     swap = [(i, i ^ 1) for i in range(masses)]
-    held = [rows] + [
+    far = [
         lax.ppermute(rows, "mass", [(i, (i + d) % masses) for i in range(masses)])
         for d in range(2, masses, 2)
     ]
-    held = held + [lax.ppermute(part, "mass", swap) for part in held]
+    near = [rows, lax.ppermute(rows, "mass", swap)]
+    far = far + [lax.ppermute(part, "mass", swap) for part in far]
     mass, seq = [lax.axis_index(axis).astype(jnp.int32).reshape(1) for axis in ("mass", "seq")]
-    side, subs = turn(mass, held)
-    pieces = score(zs, seq, side, subs, blocks)[:, None, :]
+    pieces = score(zs, seq, [turn(mass, near), turn(mass, far)], blocks)[:, None, :]
     pieces = lax.all_to_all(pieces, "seq", split_axis=0, concat_axis=0, tiled=True)[:, 0, :]
     return finish(query_bin, pieces)
 

time: 76.7 us -> 75.8 us (0.988)
  waiting for transfers between devices: 9.78 us -> 8.52 us
    ppermute x4, waiting for transfers between devices: 1.36 us -> 0.08 us  [the longest x3 0.08 us: local(): far = far + [lax.ppermute(part, 'mass', swap) for part in far]]
  transfers between devices with their start and end apart: 11 -> 11, of which waited for: 4 -> 3; matrix products, arithmetic and copies ran while one was open for 0% -> 0% of each run, Pallas kernels for 28% -> 29%
where the time goes in v2:
time: 75.8 us; the launch traced here: 74.6 us
  Pallas kernels  27.5 us (36%)
  starting transfers between devices  24 us (32%)
  blocking collectives  12.8 us (17%)
  waiting for transfers between devices  8.52 us (11%)
  local copies, waits for them, and re-layouts  0.9 us (1%)
    pallas_call x2, Pallas kernels, predict_rows(): pl.pallas_call(functools.partial(predict_kernel, part * peps), grid_spec=...  21.1 us
    all_to_all x1, blocking collectives, local(): lax.all_to_all(pieces, 'seq', split_axis=0, concat_axis=0, tiled=True)  12.8 us
    all_to_all x1, starting transfers between devices, local(): lax.all_to_all(queries, 'seq', split_axis=0, concat_axis=0, tiled=True, a...  9.03 us
    all_to_all x1, waiting for transfers between devices, local(): lax.all_to_all(queries, 'seq', split_axis=0, concat_axis=0, tiled=True, a...  7.4 us
    ppermute x3, starting transfers between devices, local(): lax.ppermute(rows, 'mass', [(i, (i + d) % masses) for i in range(masses)])  4.82 us
    ppermute x3, starting transfers between devices, local(): far = far + [lax.ppermute(part, 'mass', swap) for part in far]  3.73 us
    ppermute x1, starting transfers between devices, local(): near = [rows, lax.ppermute(rows, 'mass', swap)]  2.78 us
    pallas_call x1, Pallas kernels, score(): pl.pallas_call(functools.partial(score_kernel, zs, len(sides)), in_specs=...  2.58 us
  transfers between devices with their start and end apart: 11, of which 3 were waited for; matrix products, arithmetic and copies ran while one was open for 0% of the time, Pallas kernels for 29%

profile of v2, /device:TPU:1, one launch (start us, length us, event | category | flops | bytes accessed | tf_op | source)
XLA Modules:
  0.0 74.6 jit_solution(12412710180368545091)
XLA Ops:
  0.6 2.1 %prepare.1 = bf16[8,32,1024]{2,1,0:T(8,128)(2,1)} custom-call(s32[1,32]{1,0:T(1,128)} %bitcast.19, bf16[32,1024]{1,0:T(8,128)(2,1)} %spectra_ref.1), custom_call_target="tpu_custom_call" | custom-call | tf_op jit(solution)/shard_map/prepare/pallas_call | solution.py:383
  2.7 9.0 %all-to-all-start = ((bf16[8,32,1024]{2,1,0:T(8,128)(2,1)}), bf16[8,32,1024]{2,1,0:T(8,128)(2,1)S(1)}, u32[]{:S(2)}, u32[]{:S(2)}) async-start(bf16[8,32,1024]{2,1,0:T(8,128)(2,1)} %prepare.1), calls=%async_computation | async-start | bytes 1048576 | tf_op jit(solution)/shard_map/all_to_all | solution.py:518
  11.7 10.6 %predict.2.refs_0_ = bf16[64,1024]{1,0:T(8,128)(2,1)} custom-call(s32[64]{0:T(128)} %lengths_ref.2, s32[64]{0:T(128)} %bitcast.25, s32[64]{0:T(128)} %tsub_ref.3, s32[64]{0:T(128)} %bitcast.27, s32[64]{0:T(128)} %dsub_ref.3, s32[32,64]{1,0:T(8,128)} %bitcast.21, bf16[32,256]{1,0:T(8,128)(2,1)} %embedding_ref.3, f32[32,256]{1,0:T(8,128)} %constant.11.clone.code_ref, ...), custom_call_target="tpu_custom_call" | custom-call | flops 3221225472 | bytes 4194304 | tf_op jit(solution)/shard_map/predict/pallas_call | solution.py:344
  22.3 7.4 %all-to-all-done = bf16[8,32,1024]{2,1,0:T(8,128)(2,1)S(1)} async-done(((bf16[8,32,1024]{2,1,0:T(8,128)(2,1)}), bf16[8,32,1024]{2,1,0:T(8,128)(2,1)S(1)}, u32[]{:S(2)}, u32[]{:S(2)}) %all-to-all-start) | async-done | bytes 524320 | tf_op jit(solution)/shard_map/all_to_all | solution.py:518
  29.7 1.3 %collective-permute-start = (bf16[256,1024]{1,0:T(8,128)(2,1)S(1)}, bf16[256,1024]{1,0:T(8,128)(2,1)S(1)}, u32[]{:S(2)}, u32[]{:S(2)}) collective-permute-start(bf16[256,1024]{1,0:T(8,128)(2,1)S(1)} %bitcast.14), channel_id=1, source_target_pairs={{0,8},{1,9},{2,10},{3,11},{4,12},{5,13},{6,14},{7,15},{8,16},{9,17... | collective-permute-start | bytes 1572872 | tf_op jit(solution)/shard_map/ppermute | solution.py:524
  31.0 1.4 %collective-permute-start.1 = (bf16[256,1024]{1,0:T(8,128)(2,1)S(1)}, bf16[256,1024]{1,0:T(8,128)(2,1)S(1)}, u32[]{:S(2)}, u32[]{:S(2)}) collective-permute-start(bf16[256,1024]{1,0:T(8,128)(2,1)S(1)} %bitcast.15), channel_id=1, source_target_pairs={{0,24},{1,25},{2,26},{3,27},{4,28},{5,29},{6,30},{7,31},{8,0},{9,1... | collective-permute-start | bytes 1572872 | tf_op jit(solution)/shard_map/ppermute | solution.py:524
  32.4 10.6 %predict.3.refs_0_ = bf16[64,1024]{1,0:T(8,128)(2,1)} custom-call(s32[64]{0:T(128)} %lengths_ref.2, s32[64]{0:T(128)} %bitcast.26, s32[64]{0:T(128)} %tsub_ref.3, s32[64]{0:T(128)} %bitcast.28, s32[64]{0:T(128)} %dsub_ref.3, s32[32,64]{1,0:T(8,128)} %bitcast.22, bf16[32,256]{1,0:T(8,128)(2,1)} %embedding_ref.3, ...), custom_call_target="tpu_custom_call", output_to_operand_aliasing={{}: (15, {})} | custom-call | flops 3221225472 | bytes 4194304 | tf_op jit(solution)/shard_map/predict/pallas_call | solution.py:344
  43.0 1.0 %collective-permute-done.refs_5_ = bf16[256,1024]{1,0:T(8,128)(2,1)S(1)} collective-permute-done((bf16[256,1024]{1,0:T(8,128)(2,1)S(1)}, bf16[256,1024]{1,0:T(8,128)(2,1)S(1)}, u32[]{:S(2)}, u32[]{:S(2)}) %collective-permute-start) | collective-permute-done | bytes 524320 | tf_op jit(solution)/shard_map/ppermute | solution.py:524
  44.0 0.0 collective-permute-done.1.refs_7_
  44.0 0.9 %collective-permute-start.9 = (bf16[256,1024]{1,0:T(8,128)(2,1)S(1)}, bf16[256,1024]{1,0:T(8,128)(2,1)S(1)}, u32[]{:S(2)}, u32[]{:S(2)}) collective-permute-start(bf16[256,1024]{1,0:T(8,128)(2,1)S(1)} %collective-permute-done.refs_5_), channel_id=1, source_target_pairs={{0,8},{1,9},{2,10},{3,11},{4,12},{5,13},{6,14},{7,15},{8,16},{9,17... | collective-permute-start | bytes 1572872 | tf_op jit(solution)/shard_map/ppermute | solution.py:527
  45.0 1.2 %collective-permute-start.3 = (bf16[64,1024]{1,0:T(8,128)(2,1)}, bf16[64,1024]{1,0:T(8,128)(2,1)S(1)}, u32[]{:S(2)}, u32[]{:S(2)}) collective-permute-start(bf16[64,1024]{1,0:T(8,128)(2,1)} %predict.3.refs_0_), channel_id=1, source_target_pairs={{0,64},{32,96},{64,128},{96,160},{128,192},{160,224},{192,0},{224,... | collective-permute-start | bytes 393224 | tf_op jit(solution)/shard_map/ppermute | solution.py:531
  46.2 2.4 %collective-permute-start.4 = (bf16[64,1024]{1,0:T(8,128)(2,1)}, bf16[64,1024]{1,0:T(8,128)(2,1)S(1)}, u32[]{:S(2)}, u32[]{:S(2)}) collective-permute-start(bf16[64,1024]{1,0:T(8,128)(2,1)} %predict.3.refs_0_), channel_id=1, source_target_pairs={{0,128},{32,160},{64,192},{96,224},{128,0},{160,32},{192,64},{224,... | collective-permute-start | bytes 393224 | tf_op jit(solution)/shard_map/ppermute | solution.py:531
  48.6 1.2 %collective-permute-start.5 = (bf16[64,1024]{1,0:T(8,128)(2,1)}, bf16[64,1024]{1,0:T(8,128)(2,1)S(1)}, u32[]{:S(2)}, u32[]{:S(2)}) collective-permute-start(bf16[64,1024]{1,0:T(8,128)(2,1)} %predict.3.refs_0_), channel_id=1, source_target_pairs={{0,192},{32,224},{64,0},{96,32},{128,64},{160,96},{192,128},{224,1... | collective-permute-start | bytes 393224 | tf_op jit(solution)/shard_map/ppermute | solution.py:531
  49.8 2.8 %collective-permute-start.2 = (bf16[64,1024]{1,0:T(8,128)(2,1)}, bf16[64,1024]{1,0:T(8,128)(2,1)S(1)}, u32[]{:S(2)}, u32[]{:S(2)}) collective-permute-start(bf16[64,1024]{1,0:T(8,128)(2,1)} %predict.3.refs_0_), channel_id=1, source_target_pairs={{0,32},{32,0},{64,96},{96,64},{128,160},{160,128},{192,224},{224,1... | collective-permute-start | bytes 393224 | tf_op jit(solution)/shard_map/ppermute | solution.py:534
  52.6 0.0 collective-permute-done.3.refs_0_
  52.6 2.1 %collective-permute-start.6 = (bf16[64,1024]{1,0:T(8,128)(2,1)S(1)}, bf16[64,1024]{1,0:T(8,128)(2,1)S(1)}, u32[]{:S(2)}, u32[]{:S(2)}) collective-permute-start(bf16[64,1024]{1,0:T(8,128)(2,1)S(1)} %collective-permute-done.3.refs_0_), channel_id=1, source_target_pairs={{0,32},{32,0},{64,96},{96,64},{128,160},{160,128},{192,224},{224,1... | collective-permute-start | bytes 393224 | tf_op jit(solution)/shard_map/ppermute | solution.py:535
  54.7 0.0 collective-permute-done.4.refs_1_
  54.7 1.4 %collective-permute-start.7 = (bf16[64,1024]{1,0:T(8,128)(2,1)S(1)}, bf16[64,1024]{1,0:T(8,128)(2,1)S(1)}, u32[]{:S(2)}, u32[]{:S(2)}) collective-permute-start(bf16[64,1024]{1,0:T(8,128)(2,1)S(1)} %collective-permute-done.4.refs_1_), channel_id=1, source_target_pairs={{0,32},{32,0},{64,96},{96,64},{128,160},{160,128},{192,224},{224,1... | collective-permute-start | bytes 393224 | tf_op jit(solution)/shard_map/ppermute | solution.py:535
  56.1 0.0 collective-permute-done.5.refs_2_
  56.1 0.2 collective-permute-start.8
  56.3 0.0 collective-permute-done.2.refs_1_
  56.3 0.0 copy-start
  56.3 0.9 %copy-done = bf16[64,1024]{1,0:T(8,128)(2,1)S(1)} copy-done((bf16[64,1024]{1,0:T(8,128)(2,1)S(1)}, bf16[64,1024]{1,0:T(8,128)(2,1)}, u32[]{:S(2)}) %copy-start) | copy-done | bytes 131096
  57.2 0.1 turn.2
  57.3 0.0 collective-permute-done.6.refs_3_
  57.4 0.0 collective-permute-done.7.refs_4_
  57.4 0.1 collective-permute-done.8.refs_5_
  57.4 0.3 turn.3
  57.7 0.0 collective-permute-done.9.refs_6_
  57.7 2.6 %score.1 = f32[32,128]{1,0:T(8,128)S(1)} custom-call(s32[1]{0:T(128)} %bitcast.1.seq_ref, bf16[1024,256]{1,0:T(8,128)(2,1)S(1)} %get-tuple-element.18.refs_0_, f32[8,256]{1,0:T(8,128)S(1)} %get-tuple-element.19.refs_1_, bf16[1024,768]{1,0:T(8,128)(2,1)S(1)} %get-tuple-element.20.refs_2_, f32[8,768]{1,0:T(8,128)S(1)} %get-tuple-element.21.refs_3_, ...), custom_call_target="tpu_custom_call" | custom-call | tf_op jit(solution)/shard_map/score/pallas_call | solution.py:465
  60.3 12.8 %all_to_all.10 = f32[32,1,128]{2,1,0:T(1,128)} all-to-all(f32[32,1,128]{2,1,0:T(1,128)S(1)} %bitcast.17), channel_id=1, replica_groups=mesh['mass'=8,'seq'=32] {'seq'}, dimensions={0} | all-to-all | bytes 32768 | tf_op jit(solution)/shard_map/all_to_all | solution.py:538
  73.1 1.4 %finish.1 = (f32[1,32]{1,0:T(1,128)}, f32[1,32]{1,0:T(1,128)}) custom-call(s32[1,32]{1,0:T(1,128)} %bitcast.20, f32[32,128]{1,0:T(8,128)} %bitcast.18), custom_call_target="tpu_custom_call" | custom-call | tf_op jit(solution)/shard_map/finish/pallas_call | solution.py:488
Async XLA Ops:
  2.7 27.0 %all-to-all-start = ((bf16[8,32,1024]{2,1,0:T(8,128)(2,1)}), bf16[8,32,1024]{2,1,0:T(8,128)(2,1)S(1)}, u32[]{:S(2)}, u32[]{:S(2)}) async-start(bf16[8,32,1024]{2,1,0:T(8,128)(2,1)} %prepare.1), calls=%async_computation | async-start | bytes 1048576 | tf_op jit(solution)/shard_map/all_to_all | solution.py:518
  29.7 14.3 %collective-permute-start = (bf16[256,1024]{1,0:T(8,128)(2,1)S(1)}, bf16[256,1024]{1,0:T(8,128)(2,1)S(1)}, u32[]{:S(2)}, u32[]{:S(2)}) collective-permute-start(bf16[256,1024]{1,0:T(8,128)(2,1)S(1)} %bitcast.14), channel_id=1, source_target_pairs={{0,8},{1,9},{2,10},{3,11},{4,12},{5,13},{6,14},{7,15},{8,16},{9,17... | collective-permute-start | bytes 1572872 | tf_op jit(solution)/shard_map/ppermute | solution.py:524
  31.0 13.0 %collective-permute-start.1 = (bf16[256,1024]{1,0:T(8,128)(2,1)S(1)}, bf16[256,1024]{1,0:T(8,128)(2,1)S(1)}, u32[]{:S(2)}, u32[]{:S(2)}) collective-permute-start(bf16[256,1024]{1,0:T(8,128)(2,1)S(1)} %bitcast.15), channel_id=1, source_target_pairs={{0,24},{1,25},{2,26},{3,27},{4,28},{5,29},{6,30},{7,31},{8,0},{9,1... | collective-permute-start | bytes 1572872 | tf_op jit(solution)/shard_map/ppermute | solution.py:524
  44.0 13.7 %collective-permute-start.9 = (bf16[256,1024]{1,0:T(8,128)(2,1)S(1)}, bf16[256,1024]{1,0:T(8,128)(2,1)S(1)}, u32[]{:S(2)}, u32[]{:S(2)}) collective-permute-start(bf16[256,1024]{1,0:T(8,128)(2,1)S(1)} %collective-permute-done.refs_5_), channel_id=1, source_target_pairs={{0,8},{1,9},{2,10},{3,11},{4,12},{5,13},{6,14},{7,15},{8,16},{9,17... | collective-permute-start | bytes 1572872 | tf_op jit(solution)/shard_map/ppermute | solution.py:527
  45.0 7.6 %collective-permute-start.3 = (bf16[64,1024]{1,0:T(8,128)(2,1)}, bf16[64,1024]{1,0:T(8,128)(2,1)S(1)}, u32[]{:S(2)}, u32[]{:S(2)}) collective-permute-start(bf16[64,1024]{1,0:T(8,128)(2,1)} %predict.3.refs_0_), channel_id=1, source_target_pairs={{0,64},{32,96},{64,128},{96,160},{128,192},{160,224},{192,0},{224,... | collective-permute-start | bytes 393224 | tf_op jit(solution)/shard_map/ppermute | solution.py:531
  46.2 8.5 %collective-permute-start.4 = (bf16[64,1024]{1,0:T(8,128)(2,1)}, bf16[64,1024]{1,0:T(8,128)(2,1)S(1)}, u32[]{:S(2)}, u32[]{:S(2)}) collective-permute-start(bf16[64,1024]{1,0:T(8,128)(2,1)} %predict.3.refs_0_), channel_id=1, source_target_pairs={{0,128},{32,160},{64,192},{96,224},{128,0},{160,32},{192,64},{224,... | collective-permute-start | bytes 393224 | tf_op jit(solution)/shard_map/ppermute | solution.py:531
  48.6 7.5 %collective-permute-start.5 = (bf16[64,1024]{1,0:T(8,128)(2,1)}, bf16[64,1024]{1,0:T(8,128)(2,1)S(1)}, u32[]{:S(2)}, u32[]{:S(2)}) collective-permute-start(bf16[64,1024]{1,0:T(8,128)(2,1)} %predict.3.refs_0_), channel_id=1, source_target_pairs={{0,192},{32,224},{64,0},{96,32},{128,64},{160,96},{192,128},{224,1... | collective-permute-start | bytes 393224 | tf_op jit(solution)/shard_map/ppermute | solution.py:531
  49.8 6.5 %collective-permute-start.2 = (bf16[64,1024]{1,0:T(8,128)(2,1)}, bf16[64,1024]{1,0:T(8,128)(2,1)S(1)}, u32[]{:S(2)}, u32[]{:S(2)}) collective-permute-start(bf16[64,1024]{1,0:T(8,128)(2,1)} %predict.3.refs_0_), channel_id=1, source_target_pairs={{0,32},{32,0},{64,96},{96,64},{128,160},{160,128},{192,224},{224,1... | collective-permute-start | bytes 393224 | tf_op jit(solution)/shard_map/ppermute | solution.py:534
  52.6 4.8 %collective-permute-start.6 = (bf16[64,1024]{1,0:T(8,128)(2,1)S(1)}, bf16[64,1024]{1,0:T(8,128)(2,1)S(1)}, u32[]{:S(2)}, u32[]{:S(2)}) collective-permute-start(bf16[64,1024]{1,0:T(8,128)(2,1)S(1)} %collective-permute-done.3.refs_0_), channel_id=1, source_target_pairs={{0,32},{32,0},{64,96},{96,64},{128,160},{160,128},{192,224},{224,1... | collective-permute-start | bytes 393224 | tf_op jit(solution)/shard_map/ppermute | solution.py:535
  54.7 2.7 %collective-permute-start.7 = (bf16[64,1024]{1,0:T(8,128)(2,1)S(1)}, bf16[64,1024]{1,0:T(8,128)(2,1)S(1)}, u32[]{:S(2)}, u32[]{:S(2)}) collective-permute-start(bf16[64,1024]{1,0:T(8,128)(2,1)S(1)} %collective-permute-done.4.refs_1_), channel_id=1, source_target_pairs={{0,32},{32,0},{64,96},{96,64},{128,160},{160,128},{192,224},{224,1... | collective-permute-start | bytes 393224 | tf_op jit(solution)/shard_map/ppermute | solution.py:535
  56.1 1.3 %collective-permute-start.8 = (bf16[64,1024]{1,0:T(8,128)(2,1)S(1)}, bf16[64,1024]{1,0:T(8,128)(2,1)S(1)}, u32[]{:S(2)}, u32[]{:S(2)}) collective-permute-start(bf16[64,1024]{1,0:T(8,128)(2,1)S(1)} %collective-permute-done.5.refs_2_), channel_id=1, source_target_pairs={{0,32},{32,0},{64,96},{96,64},{128,160},{160,128},{192,224},{224,1... | collective-permute-start | bytes 393224 | tf_op jit(solution)/shard_map/ppermute | solution.py:535
  56.3 0.9 %copy-start = (bf16[64,1024]{1,0:T(8,128)(2,1)S(1)}, bf16[64,1024]{1,0:T(8,128)(2,1)}, u32[]{:S(2)}) copy-start(bf16[64,1024]{1,0:T(8,128)(2,1)} %predict.3.refs_0_) | copy-start | bytes 393220

commit v3 on v2

--- a/solution.py
+++ b/solution.py
@@ -427,17 +427,19 @@
     )(mass, *sources)
 
 
-def score_kernel(zs, sides, seq_ref, *refs):
-    turned, blocks, out_ref = refs[: 2 * sides], refs[2 * sides : -1], refs[-1]
+def score_kernel(ys, zs, jobs, sides, seq_ref, *refs):
+    turned, out_ref = refs[: 2 * sides], refs[-1]
+    blocks, rest = refs[2 * sides : 2 * sides + len(jobs)], refs[2 * sides + len(jobs) : -1]
     y = lax.div(seq_ref[0], zs)
     low, row = lane_iota((8, 128)) < 32, row_iota((8, 128))
-    for back, block in enumerate(blocks):
+    for (back, which, more), block in zip(jobs, blocks):
         queries = block[...]
         count = queries.shape[0]
-        there = lax.rem(y + len(blocks) - back, len(blocks))
+        there = lax.rem(y + ys - back, ys)
         bins = (row_iota((count, 128)) // QPB + there * (count // QPB)).astype(F32)
         tops = [jnp.zeros((count, 128), F32) for _ in range(2)]
-        for side_ref, subs_ref in zip(turned[0::2], turned[1::2]):
+        for side in which:
+            side_ref, subs_ref = turned[2 * side : 2 * side + 2]
             scores = jnp.dot(queries, side_ref[...], preferred_element_type=F32)
             tiles = scores.shape[1] // 128
             for i in range(tiles):
@@ -456,20 +458,24 @@
             near = pltpu.roll(pair[0], (128 - shift) % 128, 1)
             far = pltpu.roll(pair[1], (128 - shift + 32) % 128, 1)
             out = jnp.where(row == z, jnp.where(low, near, far), out)
-        out_ref[pl.ds(pl.multiple_of(there * zs, 8), zs), :] = out
-
-
-def score(zs, seq, sides, blocks):
+        place = pl.ds(pl.multiple_of(there * zs, 8), zs)
+        if more:
+            out = jnp.maximum(out, rest[0][place, :])
+        out_ref[place, :] = out
+
+
+def score(ys, zs, seq, sides, blocks, jobs, rest=()):
     inside = pl.BlockSpec(memory_space=pltpu.VMEM)
-    queries = len(blocks) * blocks[0].shape[0]
+    used = [blocks[job[0]] for job in jobs]
     return pl.pallas_call(
-        functools.partial(score_kernel, zs, len(sides)),
-        in_specs=[pl.BlockSpec(memory_space=pltpu.SMEM)] + [inside] * (2 * len(sides) + len(blocks)),
+        functools.partial(score_kernel, ys, zs, jobs, len(sides)),
+        in_specs=[pl.BlockSpec(memory_space=pltpu.SMEM)]
+        + [inside] * (2 * len(sides) + len(used) + len(rest)),
         out_specs=inside,
-        out_shape=jax.ShapeDtypeStruct((queries // 32, 128), F32),
+        out_shape=jax.ShapeDtypeStruct((ys * zs, 128), F32),
         compiler_params=pltpu.CompilerParams(vmem_limit_bytes=32 * 1024 * 1024),
         name="score",
-    )(seq, *[part for side in sides for part in side], *blocks)
+    )(seq, *[part for side in sides for part in side], *used, *rest)
 
 
 def finish_kernel(bins_ref, pieces_ref, target_ref, decoy_ref):
@@ -531,10 +537,13 @@
         lax.ppermute(rows, "mass", [(i, (i + d) % masses) for i in range(masses)])
         for d in range(2, masses, 2)
     ]
-    near = [rows, lax.ppermute(rows, "mass", swap)]
-    far = far + [lax.ppermute(part, "mass", swap) for part in far]
     mass, seq = [lax.axis_index(axis).astype(jnp.int32).reshape(1) for axis in ("mass", "seq")]
-    pieces = score(zs, seq, [turn(mass, near), turn(mass, far)], blocks)[:, None, :]
+    near = [rows, lax.ppermute(rows, "mass", swap), far[0], lax.ppermute(far[0], "mass", swap)]
+    near = turn(mass, near)
+    half = score(ys, zs, seq, [near], blocks, [(0, (0,), False), (1, (0,), False), (3, (0,), False)])
+    far = turn(mass, far[1:] + [lax.ppermute(part, "mass", swap) for part in far[1:]])
+    jobs = [(0, (1,), True), (1, (1,), True), (2, (0, 1), False), (3, (1,), True)]
+    pieces = score(ys, zs, seq, [near, far], blocks, jobs, [half])[:, None, :]
     pieces = lax.all_to_all(pieces, "seq", split_axis=0, concat_axis=0, tiled=True)[:, 0, :]
     return finish(query_bin, pieces)
 

time: 75.8 us -> 75.1 us (level)
    pallas_call x1 -> x2, Pallas kernels: 2.58 us -> 2.81 us  [score(): pl.pallas_call(functools.partial(score_kernel, ys, zs, jobs, len(sides)),...]
  transfers between devices with their start and end apart: 11 -> 11, of which waited for: 3 -> 2; matrix products, arithmetic and copies ran while one was open for 0% -> 0% of each run, Pallas kernels for 29% -> 30%
where the time goes in v3:
time: 75.1 us; the launch traced here: 74.6 us
  Pallas kernels  27.8 us (37%)
  starting transfers between devices  24 us (32%)
  blocking collectives  12.7 us (17%)
  waiting for transfers between devices  8.45 us (11%)
  local copies, waits for them, and re-layouts  0.9 us (1%)
    pallas_call x2, Pallas kernels, predict_rows(): pl.pallas_call(functools.partial(predict_kernel, part * peps), grid_spec=...  21.1 us
    all_to_all x1, blocking collectives, local(): lax.all_to_all(pieces, 'seq', split_axis=0, concat_axis=0, tiled=True)  12.7 us
    all_to_all x1, starting transfers between devices, local(): lax.all_to_all(queries, 'seq', split_axis=0, concat_axis=0, tiled=True, a...  9.03 us
    all_to_all x1, waiting for transfers between devices, local(): lax.all_to_all(queries, 'seq', split_axis=0, concat_axis=0, tiled=True, a...  7.4 us
    ppermute x3, starting transfers between devices, local(): lax.ppermute(rows, 'mass', [(i, (i + d) % masses) for i in range(masses)])  4.82 us
    pallas_call x2, Pallas kernels, score(): pl.pallas_call(functools.partial(score_kernel, ys, zs, jobs, len(sides)),...  2.81 us
    ppermute x1, starting transfers between devices, local(): lax.ppermute(rows, 'mass', swap)  2.78 us
    ppermute x1, starting transfers between devices, local(): lax.ppermute(far[0], 'mass', swap)  2.12 us
  transfers between devices with their start and end apart: 11, of which 2 were waited for; matrix products, arithmetic and copies ran while one was open for 0% of the time, Pallas kernels for 30%

profile of v3, /device:TPU:1, one launch (start us, length us, event | category | flops | bytes accessed | tf_op | source)
XLA Modules:
  0.0 74.6 jit_solution(3675039577414787225)
XLA Ops:
  0.6 2.1 %prepare.1 = bf16[8,32,1024]{2,1,0:T(8,128)(2,1)} custom-call(s32[1,32]{1,0:T(1,128)} %bitcast.20, bf16[32,1024]{1,0:T(8,128)(2,1)} %spectra_ref.1), custom_call_target="tpu_custom_call" | custom-call | tf_op jit(solution)/shard_map/prepare/pallas_call | solution.py:383
  2.7 9.0 %all-to-all-start = ((bf16[8,32,1024]{2,1,0:T(8,128)(2,1)}), bf16[8,32,1024]{2,1,0:T(8,128)(2,1)S(1)}, u32[]{:S(2)}, u32[]{:S(2)}) async-start(bf16[8,32,1024]{2,1,0:T(8,128)(2,1)} %prepare.1), calls=%async_computation | async-start | bytes 1048576 | tf_op jit(solution)/shard_map/all_to_all | solution.py:524
  11.7 10.6 %predict.2.refs_0_ = bf16[64,1024]{1,0:T(8,128)(2,1)} custom-call(s32[64]{0:T(128)} %lengths_ref.2, s32[64]{0:T(128)} %bitcast.26, s32[64]{0:T(128)} %tsub_ref.3, s32[64]{0:T(128)} %bitcast.28, s32[64]{0:T(128)} %dsub_ref.3, s32[32,64]{1,0:T(8,128)} %bitcast.22, bf16[32,256]{1,0:T(8,128)(2,1)} %embedding_ref.3, f32[32,256]{1,0:T(8,128)} %constant.11.clone.code_ref, ...), custom_call_target="tpu_custom_call" | custom-call | flops 3221225472 | bytes 4194304 | tf_op jit(solution)/shard_map/predict/pallas_call | solution.py:344
  22.3 7.4 %all-to-all-done = bf16[8,32,1024]{2,1,0:T(8,128)(2,1)S(1)} async-done(((bf16[8,32,1024]{2,1,0:T(8,128)(2,1)}), bf16[8,32,1024]{2,1,0:T(8,128)(2,1)S(1)}, u32[]{:S(2)}, u32[]{:S(2)}) %all-to-all-start) | async-done | bytes 524320 | tf_op jit(solution)/shard_map/all_to_all | solution.py:524
  29.7 1.3 %collective-permute-start = (bf16[256,1024]{1,0:T(8,128)(2,1)S(1)}, bf16[256,1024]{1,0:T(8,128)(2,1)S(1)}, u32[]{:S(2)}, u32[]{:S(2)}) collective-permute-start(bf16[256,1024]{1,0:T(8,128)(2,1)S(1)} %bitcast.14), channel_id=1, source_target_pairs={{0,8},{1,9},{2,10},{3,11},{4,12},{5,13},{6,14},{7,15},{8,16},{9,17... | collective-permute-start | bytes 1572872 | tf_op jit(solution)/shard_map/ppermute | solution.py:530
  31.0 1.4 %collective-permute-start.1 = (bf16[256,1024]{1,0:T(8,128)(2,1)S(1)}, bf16[256,1024]{1,0:T(8,128)(2,1)S(1)}, u32[]{:S(2)}, u32[]{:S(2)}) collective-permute-start(bf16[256,1024]{1,0:T(8,128)(2,1)S(1)} %bitcast.15), channel_id=1, source_target_pairs={{0,24},{1,25},{2,26},{3,27},{4,28},{5,29},{6,30},{7,31},{8,0},{9,1... | collective-permute-start | bytes 1572872 | tf_op jit(solution)/shard_map/ppermute | solution.py:530
  32.4 10.6 %predict.3.refs_0_ = bf16[64,1024]{1,0:T(8,128)(2,1)} custom-call(s32[64]{0:T(128)} %lengths_ref.2, s32[64]{0:T(128)} %bitcast.27, s32[64]{0:T(128)} %tsub_ref.3, s32[64]{0:T(128)} %bitcast.29, s32[64]{0:T(128)} %dsub_ref.3, s32[32,64]{1,0:T(8,128)} %bitcast.23, bf16[32,256]{1,0:T(8,128)(2,1)} %embedding_ref.3, ...), custom_call_target="tpu_custom_call", output_to_operand_aliasing={{}: (15, {})} | custom-call | flops 3221225472 | bytes 4194304 | tf_op jit(solution)/shard_map/predict/pallas_call | solution.py:344
  43.0 1.0 %collective-permute-done.refs_3_.refs_5_ = bf16[256,1024]{1,0:T(8,128)(2,1)S(1)} collective-permute-done((bf16[256,1024]{1,0:T(8,128)(2,1)S(1)}, bf16[256,1024]{1,0:T(8,128)(2,1)S(1)}, u32[]{:S(2)}, u32[]{:S(2)}) %collective-permute-start) | collective-permute-done | bytes 524320 | tf_op jit(solution)/shard_map/ppermute | solution.py:530
  44.0 0.0 collective-permute-done.1.refs_4_.refs_7_
  44.0 0.9 %collective-permute-start.9 = (bf16[256,1024]{1,0:T(8,128)(2,1)S(1)}, bf16[256,1024]{1,0:T(8,128)(2,1)S(1)}, u32[]{:S(2)}, u32[]{:S(2)}) collective-permute-start(bf16[256,1024]{1,0:T(8,128)(2,1)S(1)} %collective-permute-done.refs_3_.refs_5_), channel_id=1, source_target_pairs={{0,8},{1,9},{2,10},{3,11},{4,12},{5,13},{6,14},{7,15},{8,16},{9,17... | collective-permute-start | bytes 1572872 | tf_op jit(solution)/shard_map/ppermute | solution.py:533
  45.0 1.2 %collective-permute-start.3 = (bf16[64,1024]{1,0:T(8,128)(2,1)}, bf16[64,1024]{1,0:T(8,128)(2,1)S(1)}, u32[]{:S(2)}, u32[]{:S(2)}) collective-permute-start(bf16[64,1024]{1,0:T(8,128)(2,1)} %predict.3.refs_0_), channel_id=1, source_target_pairs={{0,64},{32,96},{64,128},{96,160},{128,192},{160,224},{192,0},{224,... | collective-permute-start | bytes 393224 | tf_op jit(solution)/shard_map/ppermute | solution.py:537
  46.2 2.4 %collective-permute-start.5 = (bf16[64,1024]{1,0:T(8,128)(2,1)}, bf16[64,1024]{1,0:T(8,128)(2,1)S(1)}, u32[]{:S(2)}, u32[]{:S(2)}) collective-permute-start(bf16[64,1024]{1,0:T(8,128)(2,1)} %predict.3.refs_0_), channel_id=1, source_target_pairs={{0,128},{32,160},{64,192},{96,224},{128,0},{160,32},{192,64},{224,... | collective-permute-start | bytes 393224 | tf_op jit(solution)/shard_map/ppermute | solution.py:537
  48.6 1.2 %collective-permute-start.6 = (bf16[64,1024]{1,0:T(8,128)(2,1)}, bf16[64,1024]{1,0:T(8,128)(2,1)S(1)}, u32[]{:S(2)}, u32[]{:S(2)}) collective-permute-start(bf16[64,1024]{1,0:T(8,128)(2,1)} %predict.3.refs_0_), channel_id=1, source_target_pairs={{0,192},{32,224},{64,0},{96,32},{128,64},{160,96},{192,128},{224,1... | collective-permute-start | bytes 393224 | tf_op jit(solution)/shard_map/ppermute | solution.py:537
  49.8 2.8 %collective-permute-start.2 = (bf16[64,1024]{1,0:T(8,128)(2,1)}, bf16[64,1024]{1,0:T(8,128)(2,1)S(1)}, u32[]{:S(2)}, u32[]{:S(2)}) collective-permute-start(bf16[64,1024]{1,0:T(8,128)(2,1)} %predict.3.refs_0_), channel_id=1, source_target_pairs={{0,32},{32,0},{64,96},{96,64},{128,160},{160,128},{192,224},{224,1... | collective-permute-start | bytes 393224 | tf_op jit(solution)/shard_map/ppermute | solution.py:541
  52.6 0.0 collective-permute-done.3.refs_2_
  52.6 2.1 %collective-permute-start.4 = (bf16[64,1024]{1,0:T(8,128)(2,1)S(1)}, bf16[64,1024]{1,0:T(8,128)(2,1)S(1)}, u32[]{:S(2)}, u32[]{:S(2)}) collective-permute-start(bf16[64,1024]{1,0:T(8,128)(2,1)S(1)} %collective-permute-done.3.refs_2_), channel_id=1, source_target_pairs={{0,32},{32,0},{64,96},{96,64},{128,160},{160,128},{192,224},{224,1... | collective-permute-start | bytes 393224 | tf_op jit(solution)/shard_map/ppermute | solution.py:541
  54.7 0.0 collective-permute-done.5.refs_0_
  54.7 1.4 %collective-permute-start.7 = (bf16[64,1024]{1,0:T(8,128)(2,1)S(1)}, bf16[64,1024]{1,0:T(8,128)(2,1)S(1)}, u32[]{:S(2)}, u32[]{:S(2)}) collective-permute-start(bf16[64,1024]{1,0:T(8,128)(2,1)S(1)} %collective-permute-done.5.refs_0_), channel_id=1, source_target_pairs={{0,32},{32,0},{64,96},{96,64},{128,160},{160,128},{192,224},{224,1... | collective-permute-start | bytes 393224 | tf_op jit(solution)/shard_map/ppermute | solution.py:544
  56.1 0.0 collective-permute-done.6.refs_1_
  56.1 0.2 collective-permute-start.8
  56.3 0.0 collective-permute-done.2.refs_1_
  56.3 0.0 collective-permute-done.4.refs_3_
  56.3 0.0 copy-start
  56.3 0.9 %copy-done = bf16[64,1024]{1,0:T(8,128)(2,1)S(1)} copy-done((bf16[64,1024]{1,0:T(8,128)(2,1)S(1)}, bf16[64,1024]{1,0:T(8,128)(2,1)}, u32[]{:S(2)}) %copy-start) | copy-done | bytes 131096
  57.2 0.2 turn.2
  57.4 1.1 %score.2.refs_8_ = f32[32,128]{1,0:T(8,128)S(1)} custom-call(s32[1]{0:T(128)} %bitcast.1.seq_ref, bf16[1024,512]{1,0:T(8,128)(2,1)S(1)} %get-tuple-element.18.refs_0_, f32[8,512]{1,0:T(8,128)S(1)} %get-tuple-element.19.refs_1_, bf16[256,1024]{1,0:T(8,128)(2,1)S(1)} %bitcast.16, bf16[256,1024]{1,0:T(8,128)(2,1)S(1)} %collective-permute-done.refs_3_.refs_5_, ...), custom_call_target="tpu_custom_call" | custom-call | tf_op jit(solution)/shard_map/score/pallas_call | solution.py:470
  58.5 0.0 collective-permute-done.7.refs_2_
  58.6 0.0 collective-permute-done.8.refs_3_
  58.6 0.2 turn.3
  58.8 0.0 collective-permute-done.9.refs_6_
  58.8 1.7 %score.3 = f32[32,128]{1,0:T(8,128)S(1)} custom-call(s32[1]{0:T(128)} %bitcast.1.seq_ref, bf16[1024,512]{1,0:T(8,128)(2,1)S(1)} %get-tuple-element.18.refs_0_, f32[8,512]{1,0:T(8,128)S(1)} %get-tuple-element.19.refs_1_, bf16[1024,512]{1,0:T(8,128)(2,1)S(1)} %get-tuple-element.20.refs_2_, f32[8,512]{1,0:T(8,128)S(1)} %get-tuple-element.21.refs_3_, ...), custom_call_target="tpu_custom_call" | custom-call | tf_op jit(solution)/shard_map/score/pallas_call | solution.py:470
  60.5 12.7 %all_to_all.10 = f32[32,1,128]{2,1,0:T(1,128)} all-to-all(f32[32,1,128]{2,1,0:T(1,128)S(1)} %bitcast.18), channel_id=1, replica_groups=mesh['mass'=8,'seq'=32] {'seq'}, dimensions={0} | all-to-all | bytes 32768 | tf_op jit(solution)/shard_map/all_to_all | solution.py:547
  73.2 1.4 %finish.1 = (f32[1,32]{1,0:T(1,128)}, f32[1,32]{1,0:T(1,128)}) custom-call(s32[1,32]{1,0:T(1,128)} %bitcast.21, f32[32,128]{1,0:T(8,128)} %bitcast.19), custom_call_target="tpu_custom_call" | custom-call | tf_op jit(solution)/shard_map/finish/pallas_call | solution.py:494
Async XLA Ops:
  2.7 27.0 %all-to-all-start = ((bf16[8,32,1024]{2,1,0:T(8,128)(2,1)}), bf16[8,32,1024]{2,1,0:T(8,128)(2,1)S(1)}, u32[]{:S(2)}, u32[]{:S(2)}) async-start(bf16[8,32,1024]{2,1,0:T(8,128)(2,1)} %prepare.1), calls=%async_computation | async-start | bytes 1048576 | tf_op jit(solution)/shard_map/all_to_all | solution.py:524
  29.7 14.3 %collective-permute-start = (bf16[256,1024]{1,0:T(8,128)(2,1)S(1)}, bf16[256,1024]{1,0:T(8,128)(2,1)S(1)}, u32[]{:S(2)}, u32[]{:S(2)}) collective-permute-start(bf16[256,1024]{1,0:T(8,128)(2,1)S(1)} %bitcast.14), channel_id=1, source_target_pairs={{0,8},{1,9},{2,10},{3,11},{4,12},{5,13},{6,14},{7,15},{8,16},{9,17... | collective-permute-start | bytes 1572872 | tf_op jit(solution)/shard_map/ppermute | solution.py:530
  31.0 13.0 %collective-permute-start.1 = (bf16[256,1024]{1,0:T(8,128)(2,1)S(1)}, bf16[256,1024]{1,0:T(8,128)(2,1)S(1)}, u32[]{:S(2)}, u32[]{:S(2)}) collective-permute-start(bf16[256,1024]{1,0:T(8,128)(2,1)S(1)} %bitcast.15), channel_id=1, source_target_pairs={{0,24},{1,25},{2,26},{3,27},{4,28},{5,29},{6,30},{7,31},{8,0},{9,1... | collective-permute-start | bytes 1572872 | tf_op jit(solution)/shard_map/ppermute | solution.py:530
  44.0 14.8 %collective-permute-start.9 = (bf16[256,1024]{1,0:T(8,128)(2,1)S(1)}, bf16[256,1024]{1,0:T(8,128)(2,1)S(1)}, u32[]{:S(2)}, u32[]{:S(2)}) collective-permute-start(bf16[256,1024]{1,0:T(8,128)(2,1)S(1)} %collective-permute-done.refs_3_.refs_5_), channel_id=1, source_target_pairs={{0,8},{1,9},{2,10},{3,11},{4,12},{5,13},{6,14},{7,15},{8,16},{9,17... | collective-permute-start | bytes 1572872 | tf_op jit(solution)/shard_map/ppermute | solution.py:533
  45.0 7.6 %collective-permute-start.3 = (bf16[64,1024]{1,0:T(8,128)(2,1)}, bf16[64,1024]{1,0:T(8,128)(2,1)S(1)}, u32[]{:S(2)}, u32[]{:S(2)}) collective-permute-start(bf16[64,1024]{1,0:T(8,128)(2,1)} %predict.3.refs_0_), channel_id=1, source_target_pairs={{0,64},{32,96},{64,128},{96,160},{128,192},{160,224},{192,0},{224,... | collective-permute-start | bytes 393224 | tf_op jit(solution)/shard_map/ppermute | solution.py:537
  46.2 8.5 %collective-permute-start.5 = (bf16[64,1024]{1,0:T(8,128)(2,1)}, bf16[64,1024]{1,0:T(8,128)(2,1)S(1)}, u32[]{:S(2)}, u32[]{:S(2)}) collective-permute-start(bf16[64,1024]{1,0:T(8,128)(2,1)} %predict.3.refs_0_), channel_id=1, source_target_pairs={{0,128},{32,160},{64,192},{96,224},{128,0},{160,32},{192,64},{224,... | collective-permute-start | bytes 393224 | tf_op jit(solution)/shard_map/ppermute | solution.py:537
  48.6 7.5 %collective-permute-start.6 = (bf16[64,1024]{1,0:T(8,128)(2,1)}, bf16[64,1024]{1,0:T(8,128)(2,1)S(1)}, u32[]{:S(2)}, u32[]{:S(2)}) collective-permute-start(bf16[64,1024]{1,0:T(8,128)(2,1)} %predict.3.refs_0_), channel_id=1, source_target_pairs={{0,192},{32,224},{64,0},{96,32},{128,64},{160,96},{192,128},{224,1... | collective-permute-start | bytes 393224 | tf_op jit(solution)/shard_map/ppermute | solution.py:537
  49.8 6.5 %collective-permute-start.2 = (bf16[64,1024]{1,0:T(8,128)(2,1)}, bf16[64,1024]{1,0:T(8,128)(2,1)S(1)}, u32[]{:S(2)}, u32[]{:S(2)}) collective-permute-start(bf16[64,1024]{1,0:T(8,128)(2,1)} %predict.3.refs_0_), channel_id=1, source_target_pairs={{0,32},{32,0},{64,96},{96,64},{128,160},{160,128},{192,224},{224,1... | collective-permute-start | bytes 393224 | tf_op jit(solution)/shard_map/ppermute | solution.py:541
  52.6 3.7 %collective-permute-start.4 = (bf16[64,1024]{1,0:T(8,128)(2,1)S(1)}, bf16[64,1024]{1,0:T(8,128)(2,1)S(1)}, u32[]{:S(2)}, u32[]{:S(2)}) collective-permute-start(bf16[64,1024]{1,0:T(8,128)(2,1)S(1)} %collective-permute-done.3.refs_2_), channel_id=1, source_target_pairs={{0,32},{32,0},{64,96},{96,64},{128,160},{160,128},{192,224},{224,1... | collective-permute-start | bytes 393224 | tf_op jit(solution)/shard_map/ppermute | solution.py:541
  54.7 3.9 %collective-permute-start.7 = (bf16[64,1024]{1,0:T(8,128)(2,1)S(1)}, bf16[64,1024]{1,0:T(8,128)(2,1)S(1)}, u32[]{:S(2)}, u32[]{:S(2)}) collective-permute-start(bf16[64,1024]{1,0:T(8,128)(2,1)S(1)} %collective-permute-done.5.refs_0_), channel_id=1, source_target_pairs={{0,32},{32,0},{64,96},{96,64},{128,160},{160,128},{192,224},{224,1... | collective-permute-start | bytes 393224 | tf_op jit(solution)/shard_map/ppermute | solution.py:544
  56.1 2.5 %collective-permute-start.8 = (bf16[64,1024]{1,0:T(8,128)(2,1)S(1)}, bf16[64,1024]{1,0:T(8,128)(2,1)S(1)}, u32[]{:S(2)}, u32[]{:S(2)}) collective-permute-start(bf16[64,1024]{1,0:T(8,128)(2,1)S(1)} %collective-permute-done.6.refs_1_), channel_id=1, source_target_pairs={{0,32},{32,0},{64,96},{96,64},{128,160},{160,128},{192,224},{224,1... | collective-permute-start | bytes 393224 | tf_op jit(solution)/shard_map/ppermute | solution.py:544
  56.3 0.9 %copy-start = (bf16[64,1024]{1,0:T(8,128)(2,1)S(1)}, bf16[64,1024]{1,0:T(8,128)(2,1)}, u32[]{:S(2)}) copy-start(bf16[64,1024]{1,0:T(8,128)(2,1)} %predict.3.refs_0_) | copy-start | bytes 393220

commit v4 on v3

--- a/solution.py
+++ b/solution.py
@@ -474,6 +474,11 @@
         out_specs=inside,
         out_shape=jax.ShapeDtypeStruct((ys * zs, 128), F32),
         compiler_params=pltpu.CompilerParams(vmem_limit_bytes=32 * 1024 * 1024),
+        cost_estimate=pl.CostEstimate(
+            flops=sum(2 * blocks[0].size * sides[i][0].shape[1] for job in jobs for i in job[1]),
+            bytes_accessed=4 * 2**20,
+            transcendentals=0,
+        ),
         name="score",
     )(seq, *[part for side in sides for part in side], *used, *rest)
 

time: 75.1 us -> 75.2 us (level)
  no operation moved by 1% of the time
where the time goes in v4:
time: 75.2 us; the launch traced here: 74.7 us
  Pallas kernels  27.8 us (37%)
  starting transfers between devices  24 us (32%)
  blocking collectives  12.9 us (17%)
  waiting for transfers between devices  8.46 us (11%)
  local copies, waits for them, and re-layouts  0.9 us (1%)
    pallas_call x2, Pallas kernels, predict_rows(): pl.pallas_call(functools.partial(predict_kernel, part * peps), grid_spec=...  21.1 us
    all_to_all x1, blocking collectives, local(): lax.all_to_all(pieces, 'seq', split_axis=0, concat_axis=0, tiled=True)  12.9 us
    all_to_all x1, starting transfers between devices, local(): lax.all_to_all(queries, 'seq', split_axis=0, concat_axis=0, tiled=True, a...  9.03 us
    all_to_all x1, waiting for transfers between devices, local(): lax.all_to_all(queries, 'seq', split_axis=0, concat_axis=0, tiled=True, a...  7.4 us
    ppermute x3, starting transfers between devices, local(): lax.ppermute(rows, 'mass', [(i, (i + d) % masses) for i in range(masses)])  4.82 us
    pallas_call x2, Pallas kernels, score(): pl.pallas_call(functools.partial(score_kernel, ys, zs, jobs, len(sides)),...  2.81 us
    ppermute x1, starting transfers between devices, local(): lax.ppermute(rows, 'mass', swap)  2.78 us
    ppermute x1, starting transfers between devices, local(): lax.ppermute(far[0], 'mass', swap)  2.12 us
  transfers between devices with their start and end apart: 11, of which 2 were waited for; matrix products, arithmetic and copies ran while one was open for 0% of the time, Pallas kernels for 30%

profile of v4, /device:TPU:1, one launch (start us, length us, event | category | flops | bytes accessed | tf_op | source)
XLA Modules:
  0.0 74.7 jit_solution(13142732491980399797)
XLA Ops:
  0.6 2.1 %prepare.1 = bf16[8,32,1024]{2,1,0:T(8,128)(2,1)} custom-call(s32[1,32]{1,0:T(1,128)} %bitcast.20, bf16[32,1024]{1,0:T(8,128)(2,1)} %spectra_ref.1), custom_call_target="tpu_custom_call" | custom-call | tf_op jit(solution)/shard_map/prepare/pallas_call | solution.py:383
  2.7 9.0 %all-to-all-start = ((bf16[8,32,1024]{2,1,0:T(8,128)(2,1)}), bf16[8,32,1024]{2,1,0:T(8,128)(2,1)S(1)}, u32[]{:S(2)}, u32[]{:S(2)}) async-start(bf16[8,32,1024]{2,1,0:T(8,128)(2,1)} %prepare.1), calls=%async_computation | async-start | bytes 1048576 | tf_op jit(solution)/shard_map/all_to_all | solution.py:529
  11.7 10.6 %predict.2.refs_0_ = bf16[64,1024]{1,0:T(8,128)(2,1)} custom-call(s32[64]{0:T(128)} %lengths_ref.2, s32[64]{0:T(128)} %bitcast.26, s32[64]{0:T(128)} %tsub_ref.3, s32[64]{0:T(128)} %bitcast.28, s32[64]{0:T(128)} %dsub_ref.3, s32[32,64]{1,0:T(8,128)} %bitcast.22, bf16[32,256]{1,0:T(8,128)(2,1)} %embedding_ref.3, f32[32,256]{1,0:T(8,128)} %constant.11.clone.code_ref, ...), custom_call_target="tpu_custom_call" | custom-call | flops 3221225472 | bytes 4194304 | tf_op jit(solution)/shard_map/predict/pallas_call | solution.py:344
  22.3 7.4 %all-to-all-done = bf16[8,32,1024]{2,1,0:T(8,128)(2,1)S(1)} async-done(((bf16[8,32,1024]{2,1,0:T(8,128)(2,1)}), bf16[8,32,1024]{2,1,0:T(8,128)(2,1)S(1)}, u32[]{:S(2)}, u32[]{:S(2)}) %all-to-all-start) | async-done | bytes 524320 | tf_op jit(solution)/shard_map/all_to_all | solution.py:529
  29.7 1.3 %collective-permute-start = (bf16[256,1024]{1,0:T(8,128)(2,1)S(1)}, bf16[256,1024]{1,0:T(8,128)(2,1)S(1)}, u32[]{:S(2)}, u32[]{:S(2)}) collective-permute-start(bf16[256,1024]{1,0:T(8,128)(2,1)S(1)} %bitcast.14), channel_id=1, source_target_pairs={{0,8},{1,9},{2,10},{3,11},{4,12},{5,13},{6,14},{7,15},{8,16},{9,17... | collective-permute-start | bytes 1572872 | tf_op jit(solution)/shard_map/ppermute | solution.py:535
  31.0 1.4 %collective-permute-start.1 = (bf16[256,1024]{1,0:T(8,128)(2,1)S(1)}, bf16[256,1024]{1,0:T(8,128)(2,1)S(1)}, u32[]{:S(2)}, u32[]{:S(2)}) collective-permute-start(bf16[256,1024]{1,0:T(8,128)(2,1)S(1)} %bitcast.15), channel_id=1, source_target_pairs={{0,24},{1,25},{2,26},{3,27},{4,28},{5,29},{6,30},{7,31},{8,0},{9,1... | collective-permute-start | bytes 1572872 | tf_op jit(solution)/shard_map/ppermute | solution.py:535
  32.4 10.6 %predict.3.refs_0_ = bf16[64,1024]{1,0:T(8,128)(2,1)} custom-call(s32[64]{0:T(128)} %lengths_ref.2, s32[64]{0:T(128)} %bitcast.27, s32[64]{0:T(128)} %tsub_ref.3, s32[64]{0:T(128)} %bitcast.29, s32[64]{0:T(128)} %dsub_ref.3, s32[32,64]{1,0:T(8,128)} %bitcast.23, bf16[32,256]{1,0:T(8,128)(2,1)} %embedding_ref.3, ...), custom_call_target="tpu_custom_call", output_to_operand_aliasing={{}: (15, {})} | custom-call | flops 3221225472 | bytes 4194304 | tf_op jit(solution)/shard_map/predict/pallas_call | solution.py:344
  43.0 1.0 %collective-permute-done.refs_3_.refs_5_ = bf16[256,1024]{1,0:T(8,128)(2,1)S(1)} collective-permute-done((bf16[256,1024]{1,0:T(8,128)(2,1)S(1)}, bf16[256,1024]{1,0:T(8,128)(2,1)S(1)}, u32[]{:S(2)}, u32[]{:S(2)}) %collective-permute-start) | collective-permute-done | bytes 524320 | tf_op jit(solution)/shard_map/ppermute | solution.py:535
  44.0 0.0 collective-permute-done.1.refs_4_.refs_7_
  44.0 0.9 %collective-permute-start.9 = (bf16[256,1024]{1,0:T(8,128)(2,1)S(1)}, bf16[256,1024]{1,0:T(8,128)(2,1)S(1)}, u32[]{:S(2)}, u32[]{:S(2)}) collective-permute-start(bf16[256,1024]{1,0:T(8,128)(2,1)S(1)} %collective-permute-done.refs_3_.refs_5_), channel_id=1, source_target_pairs={{0,8},{1,9},{2,10},{3,11},{4,12},{5,13},{6,14},{7,15},{8,16},{9,17... | collective-permute-start | bytes 1572872 | tf_op jit(solution)/shard_map/ppermute | solution.py:538
  45.0 1.2 %collective-permute-start.3 = (bf16[64,1024]{1,0:T(8,128)(2,1)}, bf16[64,1024]{1,0:T(8,128)(2,1)S(1)}, u32[]{:S(2)}, u32[]{:S(2)}) collective-permute-start(bf16[64,1024]{1,0:T(8,128)(2,1)} %predict.3.refs_0_), channel_id=1, source_target_pairs={{0,64},{32,96},{64,128},{96,160},{128,192},{160,224},{192,0},{224,... | collective-permute-start | bytes 393224 | tf_op jit(solution)/shard_map/ppermute | solution.py:542
  46.2 2.4 %collective-permute-start.5 = (bf16[64,1024]{1,0:T(8,128)(2,1)}, bf16[64,1024]{1,0:T(8,128)(2,1)S(1)}, u32[]{:S(2)}, u32[]{:S(2)}) collective-permute-start(bf16[64,1024]{1,0:T(8,128)(2,1)} %predict.3.refs_0_), channel_id=1, source_target_pairs={{0,128},{32,160},{64,192},{96,224},{128,0},{160,32},{192,64},{224,... | collective-permute-start | bytes 393224 | tf_op jit(solution)/shard_map/ppermute | solution.py:542
  48.6 1.2 %collective-permute-start.6 = (bf16[64,1024]{1,0:T(8,128)(2,1)}, bf16[64,1024]{1,0:T(8,128)(2,1)S(1)}, u32[]{:S(2)}, u32[]{:S(2)}) collective-permute-start(bf16[64,1024]{1,0:T(8,128)(2,1)} %predict.3.refs_0_), channel_id=1, source_target_pairs={{0,192},{32,224},{64,0},{96,32},{128,64},{160,96},{192,128},{224,1... | collective-permute-start | bytes 393224 | tf_op jit(solution)/shard_map/ppermute | solution.py:542
  49.8 2.8 %collective-permute-start.2 = (bf16[64,1024]{1,0:T(8,128)(2,1)}, bf16[64,1024]{1,0:T(8,128)(2,1)S(1)}, u32[]{:S(2)}, u32[]{:S(2)}) collective-permute-start(bf16[64,1024]{1,0:T(8,128)(2,1)} %predict.3.refs_0_), channel_id=1, source_target_pairs={{0,32},{32,0},{64,96},{96,64},{128,160},{160,128},{192,224},{224,1... | collective-permute-start | bytes 393224 | tf_op jit(solution)/shard_map/ppermute | solution.py:546
  52.6 0.0 collective-permute-done.3.refs_2_
  52.6 2.1 %collective-permute-start.4 = (bf16[64,1024]{1,0:T(8,128)(2,1)S(1)}, bf16[64,1024]{1,0:T(8,128)(2,1)S(1)}, u32[]{:S(2)}, u32[]{:S(2)}) collective-permute-start(bf16[64,1024]{1,0:T(8,128)(2,1)S(1)} %collective-permute-done.3.refs_2_), channel_id=1, source_target_pairs={{0,32},{32,0},{64,96},{96,64},{128,160},{160,128},{192,224},{224,1... | collective-permute-start | bytes 393224 | tf_op jit(solution)/shard_map/ppermute | solution.py:546
  54.7 0.0 collective-permute-done.5.refs_0_
  54.7 1.4 %collective-permute-start.7 = (bf16[64,1024]{1,0:T(8,128)(2,1)S(1)}, bf16[64,1024]{1,0:T(8,128)(2,1)S(1)}, u32[]{:S(2)}, u32[]{:S(2)}) collective-permute-start(bf16[64,1024]{1,0:T(8,128)(2,1)S(1)} %collective-permute-done.5.refs_0_), channel_id=1, source_target_pairs={{0,32},{32,0},{64,96},{96,64},{128,160},{160,128},{192,224},{224,1... | collective-permute-start | bytes 393224 | tf_op jit(solution)/shard_map/ppermute | solution.py:549
  56.1 0.0 collective-permute-done.6.refs_1_
  56.1 0.2 collective-permute-start.8
  56.3 0.0 collective-permute-done.2.refs_1_
  56.3 0.0 collective-permute-done.4.refs_3_
  56.3 0.0 copy-start
  56.3 0.9 %copy-done = bf16[64,1024]{1,0:T(8,128)(2,1)S(1)} copy-done((bf16[64,1024]{1,0:T(8,128)(2,1)S(1)}, bf16[64,1024]{1,0:T(8,128)(2,1)}, u32[]{:S(2)}) %copy-start) | copy-done | bytes 131096
  57.2 0.2 turn.2
  57.4 0.0 collective-permute-done.7.refs_2_
  57.4 0.0 collective-permute-done.8.refs_3_
  57.4 0.2 turn.3
  57.6 1.1 %score.2.refs_8_ = f32[32,128]{1,0:T(8,128)S(1)} custom-call(s32[1]{0:T(128)} %bitcast.1.seq_ref, bf16[1024,512]{1,0:T(8,128)(2,1)S(1)} %get-tuple-element.18.refs_0_, f32[8,512]{1,0:T(8,128)S(1)} %get-tuple-element.19.refs_1_, bf16[256,1024]{1,0:T(8,128)(2,1)S(1)} %bitcast.16, bf16[256,1024]{1,0:T(8,128)(2,1)S(1)} %collective-permute-done.refs_3_.refs_5_, ...), custom_call_target="tpu_custom_call" | custom-call | flops 805306368 | bytes 4194304 | tf_op jit(solution)/shard_map/score/pallas_call | solution.py:470
  58.8 0.0 collective-permute-done.9.refs_6_
  58.8 1.7 %score.3 = f32[32,128]{1,0:T(8,128)S(1)} custom-call(s32[1]{0:T(128)} %bitcast.1.seq_ref, bf16[1024,512]{1,0:T(8,128)(2,1)S(1)} %get-tuple-element.18.refs_0_, f32[8,512]{1,0:T(8,128)S(1)} %get-tuple-element.19.refs_1_, bf16[1024,512]{1,0:T(8,128)(2,1)S(1)} %get-tuple-element.20.refs_2_, f32[8,512]{1,0:T(8,128)S(1)} %get-tuple-element.21.refs_3_, ...), custom_call_target="tpu_custom_call" | custom-call | flops 1342177280 | bytes 4194304 | tf_op jit(solution)/shard_map/score/pallas_call | solution.py:470
  60.5 12.9 %all_to_all.10 = f32[32,1,128]{2,1,0:T(1,128)} all-to-all(f32[32,1,128]{2,1,0:T(1,128)S(1)} %bitcast.18), channel_id=1, replica_groups=mesh['mass'=8,'seq'=32] {'seq'}, dimensions={0} | all-to-all | bytes 32768 | tf_op jit(solution)/shard_map/all_to_all | solution.py:552
  73.3 1.4 %finish.1 = (f32[1,32]{1,0:T(1,128)}, f32[1,32]{1,0:T(1,128)}) custom-call(s32[1,32]{1,0:T(1,128)} %bitcast.21, f32[32,128]{1,0:T(8,128)} %bitcast.19), custom_call_target="tpu_custom_call" | custom-call | tf_op jit(solution)/shard_map/finish/pallas_call | solution.py:499
Async XLA Ops:
  2.7 27.0 %all-to-all-start = ((bf16[8,32,1024]{2,1,0:T(8,128)(2,1)}), bf16[8,32,1024]{2,1,0:T(8,128)(2,1)S(1)}, u32[]{:S(2)}, u32[]{:S(2)}) async-start(bf16[8,32,1024]{2,1,0:T(8,128)(2,1)} %prepare.1), calls=%async_computation | async-start | bytes 1048576 | tf_op jit(solution)/shard_map/all_to_all | solution.py:529
  29.7 14.3 %collective-permute-start = (bf16[256,1024]{1,0:T(8,128)(2,1)S(1)}, bf16[256,1024]{1,0:T(8,128)(2,1)S(1)}, u32[]{:S(2)}, u32[]{:S(2)}) collective-permute-start(bf16[256,1024]{1,0:T(8,128)(2,1)S(1)} %bitcast.14), channel_id=1, source_target_pairs={{0,8},{1,9},{2,10},{3,11},{4,12},{5,13},{6,14},{7,15},{8,16},{9,17... | collective-permute-start | bytes 1572872 | tf_op jit(solution)/shard_map/ppermute | solution.py:535
  31.0 13.0 %collective-permute-start.1 = (bf16[256,1024]{1,0:T(8,128)(2,1)S(1)}, bf16[256,1024]{1,0:T(8,128)(2,1)S(1)}, u32[]{:S(2)}, u32[]{:S(2)}) collective-permute-start(bf16[256,1024]{1,0:T(8,128)(2,1)S(1)} %bitcast.15), channel_id=1, source_target_pairs={{0,24},{1,25},{2,26},{3,27},{4,28},{5,29},{6,30},{7,31},{8,0},{9,1... | collective-permute-start | bytes 1572872 | tf_op jit(solution)/shard_map/ppermute | solution.py:535
  44.0 14.8 %collective-permute-start.9 = (bf16[256,1024]{1,0:T(8,128)(2,1)S(1)}, bf16[256,1024]{1,0:T(8,128)(2,1)S(1)}, u32[]{:S(2)}, u32[]{:S(2)}) collective-permute-start(bf16[256,1024]{1,0:T(8,128)(2,1)S(1)} %collective-permute-done.refs_3_.refs_5_), channel_id=1, source_target_pairs={{0,8},{1,9},{2,10},{3,11},{4,12},{5,13},{6,14},{7,15},{8,16},{9,17... | collective-permute-start | bytes 1572872 | tf_op jit(solution)/shard_map/ppermute | solution.py:538
  45.0 7.6 %collective-permute-start.3 = (bf16[64,1024]{1,0:T(8,128)(2,1)}, bf16[64,1024]{1,0:T(8,128)(2,1)S(1)}, u32[]{:S(2)}, u32[]{:S(2)}) collective-permute-start(bf16[64,1024]{1,0:T(8,128)(2,1)} %predict.3.refs_0_), channel_id=1, source_target_pairs={{0,64},{32,96},{64,128},{96,160},{128,192},{160,224},{192,0},{224,... | collective-permute-start | bytes 393224 | tf_op jit(solution)/shard_map/ppermute | solution.py:542
  46.2 8.5 %collective-permute-start.5 = (bf16[64,1024]{1,0:T(8,128)(2,1)}, bf16[64,1024]{1,0:T(8,128)(2,1)S(1)}, u32[]{:S(2)}, u32[]{:S(2)}) collective-permute-start(bf16[64,1024]{1,0:T(8,128)(2,1)} %predict.3.refs_0_), channel_id=1, source_target_pairs={{0,128},{32,160},{64,192},{96,224},{128,0},{160,32},{192,64},{224,... | collective-permute-start | bytes 393224 | tf_op jit(solution)/shard_map/ppermute | solution.py:542
  48.6 7.5 %collective-permute-start.6 = (bf16[64,1024]{1,0:T(8,128)(2,1)}, bf16[64,1024]{1,0:T(8,128)(2,1)S(1)}, u32[]{:S(2)}, u32[]{:S(2)}) collective-permute-start(bf16[64,1024]{1,0:T(8,128)(2,1)} %predict.3.refs_0_), channel_id=1, source_target_pairs={{0,192},{32,224},{64,0},{96,32},{128,64},{160,96},{192,128},{224,1... | collective-permute-start | bytes 393224 | tf_op jit(solution)/shard_map/ppermute | solution.py:542
  49.8 6.5 %collective-permute-start.2 = (bf16[64,1024]{1,0:T(8,128)(2,1)}, bf16[64,1024]{1,0:T(8,128)(2,1)S(1)}, u32[]{:S(2)}, u32[]{:S(2)}) collective-permute-start(bf16[64,1024]{1,0:T(8,128)(2,1)} %predict.3.refs_0_), channel_id=1, source_target_pairs={{0,32},{32,0},{64,96},{96,64},{128,160},{160,128},{192,224},{224,1... | collective-permute-start | bytes 393224 | tf_op jit(solution)/shard_map/ppermute | solution.py:546
  52.6 3.7 %collective-permute-start.4 = (bf16[64,1024]{1,0:T(8,128)(2,1)S(1)}, bf16[64,1024]{1,0:T(8,128)(2,1)S(1)}, u32[]{:S(2)}, u32[]{:S(2)}) collective-permute-start(bf16[64,1024]{1,0:T(8,128)(2,1)S(1)} %collective-permute-done.3.refs_2_), channel_id=1, source_target_pairs={{0,32},{32,0},{64,96},{96,64},{128,160},{160,128},{192,224},{224,1... | collective-permute-start | bytes 393224 | tf_op jit(solution)/shard_map/ppermute | solution.py:546
  54.7 2.7 %collective-permute-start.7 = (bf16[64,1024]{1,0:T(8,128)(2,1)S(1)}, bf16[64,1024]{1,0:T(8,128)(2,1)S(1)}, u32[]{:S(2)}, u32[]{:S(2)}) collective-permute-start(bf16[64,1024]{1,0:T(8,128)(2,1)S(1)} %collective-permute-done.5.refs_0_), channel_id=1, source_target_pairs={{0,32},{32,0},{64,96},{96,64},{128,160},{160,128},{192,224},{224,1... | collective-permute-start | bytes 393224 | tf_op jit(solution)/shard_map/ppermute | solution.py:549
  56.1 1.3 %collective-permute-start.8 = (bf16[64,1024]{1,0:T(8,128)(2,1)S(1)}, bf16[64,1024]{1,0:T(8,128)(2,1)S(1)}, u32[]{:S(2)}, u32[]{:S(2)}) collective-permute-start(bf16[64,1024]{1,0:T(8,128)(2,1)S(1)} %collective-permute-done.6.refs_1_), channel_id=1, source_target_pairs={{0,32},{32,0},{64,96},{96,64},{128,160},{160,128},{192,224},{224,1... | collective-permute-start | bytes 393224 | tf_op jit(solution)/shard_map/ppermute | solution.py:549
  56.3 0.9 %copy-start = (bf16[64,1024]{1,0:T(8,128)(2,1)S(1)}, bf16[64,1024]{1,0:T(8,128)(2,1)}, u32[]{:S(2)}) copy-start(bf16[64,1024]{1,0:T(8,128)(2,1)} %predict.3.refs_0_) | copy-start | bytes 393220
